TPU v7x, 256 devices: a whole 4x4x8 slice. The times are simulated.
256 devices in a mesh: jpair: 8 (over z_hi, x), rows: 32 (over z_lo, y, core).
Axes of the slice: x: 4, y: 4, z: 8 (z_hi: 2, z_lo: 4; z = z_hi * 4 + z_lo), core: 2. Of those that a mesh axis runs over, the one named last changes fastest.
Arguments:
- psi_low: bfloat16 [32768, 2048], P('rows', 'jpair'), may hold values from -0.03125 to 0.03125
- psi_high: bfloat16 [32768, 2048], P('rows', 'jpair'), may hold values from -6 to 6
- dip_blocks: bfloat16 [2048, 256, 256], P('rows'), may hold values from -0.09375 to 0.09375
- block_cols: int32 [2048], replicated, may hold values from 0 to 127, as said below
Outputs:
- dipole_tile: float32 [2048, 2048], P('rows', 'jpair')
Inputs may be any that keep to these rules, and one draw needn't show every extreme that they name: `block_cols`: entries 64 * s to 64 * s + 63 are the blocks stored on row shard s; block c is stored on row shard c // 4. Among the entries of one row shard, no row shard's blocks are named more than 4 times, and some row shard's blocks are named exactly 4 times by every row shard.
All inputs are finite; a program needn't handle non-finite values.
Results may differ from a plain program's by a relative error of at most 0.0029.
Values may be sent and summed in bfloat16 or wider, within the bound.
A program may use at most 128 MiB of HBM per device.

v0:
```python
import jax
import jax.numpy as jnp
from jax import lax
from jax.sharding import PartitionSpec as P

BLK = 256
KNZ = 16


def shards(psi_low, psi_high, dip_blocks, block_cols):
    shard_count = lax.axis_size("rows")
    own_index = lax.axis_index("rows")
    rows_dev, columns = psi_high.shape
    per_dev = dip_blocks.shape[0]
    rb_dev = rows_dev // BLK
    own_list = lax.dynamic_slice_in_dim(block_cols, own_index * per_dev, per_dev)
    capacity = max(2, 2 * ((per_dev + shard_count - 1) // shard_count))
    requests = block_cols.reshape(shard_count, per_dev)
    owners = requests // rb_dev
    positions = jnp.arange(per_dev, dtype=jnp.int32)
    same_owner = owners[:, :, None] == owners[:, None, :]
    before = positions[None, None, :] < positions[None, :, None]
    slot_rank = jnp.sum(jnp.logical_and(same_owner, before), axis=2)
    slot_ids = jnp.arange(capacity, dtype=jnp.int32)
    matches = jnp.logical_and(
        (owners == own_index)[:, :, None], slot_rank[:, :, None] == slot_ids[None, None, :]
    )
    local_pick = jnp.sum(jnp.where(matches, (requests % rb_dev)[:, :, None], 0), axis=1)
    filled = jnp.any(matches, axis=1)
    own_blocks = psi_high.reshape(rb_dev, BLK, columns)
    outgoing = jnp.where(
        filled[:, :, None, None], own_blocks[local_pick], jnp.zeros((), psi_high.dtype)
    )
    incoming = lax.all_to_all(outgoing, "rows", split_axis=0, concat_axis=0, tiled=True)
    own_owner = own_list // rb_dev
    own_rank = lax.dynamic_index_in_dim(slot_rank, own_index, 0, keepdims=False)
    fetched = incoming.reshape(shard_count * capacity, BLK, columns)[
        own_owner * capacity + own_rank
    ]
    products = jnp.einsum("jab,jbc->jac", dip_blocks, fetched, preferred_element_type=jnp.float32)
    applied = (
        products.reshape(rb_dev, KNZ, BLK, columns)
        .sum(axis=1)
        .reshape(rows_dev, columns)
        .astype(jnp.bfloat16)
    )
    partial_tile = jnp.dot(
        lax.all_gather(psi_low, "jpair", axis=1, tiled=True).T,
        applied,
        preferred_element_type=jnp.float32,
    )
    return lax.psum_scatter(partial_tile, "rows", scatter_dimension=0, tiled=True)


def solution(mesh):
    placed = (P("rows", "jpair"), P("rows", "jpair"), P("rows", None, None), P())
    return jax.shard_map(
        shards, mesh=mesh, in_specs=placed, out_specs=P("rows", "jpair"), check_vma=False
    )
```

profile of v0, /device:TPU:1, one launch (start us, length us, event | category | flops | bytes accessed | tf_op | source)
XLA Modules:
  0.0 650.1 jit_solution(6893028479566461567)
XLA Ops:
  6.6 0.8 reshape.131
  7.4 0.9 convert_reduce_fusion
  8.3 0.1 fusion.1
  8.5 0.2 select_reduce_fusion
  8.7 0.1 copy.18
  8.7 0.1 reshape.137
  8.9 0.1 copy.17
  9.0 0.0 copy-done
  9.0 8.0 %gather_fusion = bf16[128,256,256]{2,1,0:T(8,128)(2,1)} fusion(bf16[4,256,256]{2,1,0:T(8,128)(2,1)S(1)} %bitcast.23, s32[1024]{0:T(1024)S(1)} %pad_clamp_fusion.1), kind=kCustom, calls=%fused_computation | custom fusion | bytes 33554944 | tf_op jit(solution)/shard_map/gather | solution.py:32
  16.9 14.0 %broadcast_select_fusion = bf16[32,4,256,256]{3,2,1,0:T(8,128)(2,1)} fusion(bf16[32,4,256,256]{3,2,1,0:T(8,128)(2,1)} %bitcast.24, pred[32,4]{1,0:T(8,128)(4,1)S(1)} %copy.17), kind=kLoop, calls=%fused_computation.3 | loop fusion | flops 8388608 | bytes 33554560 | tf_op jit(solution)/shard_map/jit(_where)/select_n | solution.py:31
  30.9 10.2 %all-to-all-start = ((bf16[32,4,256,256]{3,2,1,0:T(8,128)(2,1)}), bf16[32,4,256,256]{3,2,1,0:T(8,128)(2,1)}, u32[]{:S(2)}, u32[]{:S(2)}) async-start(bf16[32,4,256,256]{3,2,1,0:T(8,128)(2,1)} %broadcast_select_fusion), calls=%async_computation | async-start | bytes 33554432 | tf_op jit(solution)/shard_map/all_to_all | solution.py:34
  41.1 0.0 all-gather.2.cloned.1.call-start
  41.2 0.7 all-gather.2.cloned.1.call-update
  41.8 0.0 reduce-scatter.4.cloned.1.call-start
  41.9 0.8 compare_select_fusion.1
  42.7 425.7 %all-to-all-done = bf16[32,4,256,256]{3,2,1,0:T(8,128)(2,1)} async-done(((bf16[32,4,256,256]{3,2,1,0:T(8,128)(2,1)}), bf16[32,4,256,256]{3,2,1,0:T(8,128)(2,1)}, u32[]{:S(2)}, u32[]{:S(2)}) %all-to-all-start) | async-done | bytes 16777248 | tf_op jit(solution)/shard_map/all_to_all | solution.py:34
  468.4 11.3 %gather_fusion.1 = bf16[64,256,256]{2,1,0:T(8,128)(2,1)} fusion(bf16[128,256,256]{2,1,0:T(8,128)(2,1)} %bitcast.3, s32[1024]{0:T(1024)S(1)} %pad_clamp_fusion), kind=kCustom, calls=%fused_computation.1 | custom fusion | bytes 16777472 | tf_op jit(solution)/shard_map/gather | solution.py:37
  479.7 10.6 %bitcast_reduce_fusion = bf16[4,256,256]{1,2,0:T(8,128)(2,1)S(1)} fusion(bf16[64,256,256]{2,1,0:T(8,128)(2,1)} %gather_fusion.1, bf16[64,256,256]{2,1,0:T(8,128)(2,1)} %param.6), kind=kOutput, calls=%fused_computation.2 | convolution fusion | flops 2151415808 | bytes 17301504 | tf_op jit(solution)/shard_map/jab,jbc->jac/dot_general | solution.py:40
  490.3 0.2 copy.20
  490.5 0.0 all-gather.2.cloned.1.call-done
  490.6 3.5 convolution_bitcast_fusion
  494.0 1.9 copy.23
  495.9 0.0 reduce-scatter.4.cloned.1.call-update
  495.9 147.3 %reduce-scatter.4.cloned.1.call-done = f32[64,256]{1,0:T(8,128)} async-done(((f32[2048,256]{1,0:T(8,128)}), f32[64,256]{1,0:T(8,128)}) %reduce-scatter.4.cloned.1.call-update) | async-done | bytes 65552 | tf_op jit(solution)/shard_map/reduce_scatter | solution.py:52
  (9 shorter events, 0.1 us)
Async XLA Ops:
  6.5 2.4 copy-start
  30.9 437.5 %all-to-all-start = ((bf16[32,4,256,256]{3,2,1,0:T(8,128)(2,1)}), bf16[32,4,256,256]{3,2,1,0:T(8,128)(2,1)}, u32[]{:S(2)}, u32[]{:S(2)}) async-start(bf16[32,4,256,256]{3,2,1,0:T(8,128)(2,1)} %broadcast_select_fusion), calls=%async_computation | async-start | bytes 33554432 | tf_op jit(solution)/shard_map/all_to_all | solution.py:34
  41.1 449.5 %all-gather.2.cloned.1.call-start = ((), (), s32[]{:S(2)}) async-start(), calls=%async_computation.2 | async-start | bytes 4718592 | tf_op jit(solution)/shard_map/all_gather | solution.py:48
  41.8 601.4 %reduce-scatter.4.cloned.1.call-start = ((), (), s32[]{:S(2)}) async-start(), calls=%async_computation.3 | async-start | bytes 2162688 | tf_op jit(solution)/shard_map/reduce_scatter | solution.py:52
  479.7 163.5 %copy-start.1 = (bf16[1024,256]{1,0:T(8,128)(2,1)S(1)}, bf16[1024,256]{1,0:T(8,128)(2,1)}, u32[]{:S(2)}) copy-start(bf16[1024,256]{1,0:T(8,128)(2,1)} %param.5) | copy-start | bytes 1572868
Sparse Core Ops, SparseCore 0:
  44.4 165.0 all-gather.1
  496.1 147.1 reduce-scatter.3
where the time goes:
time: 655 us; the launch traced here: 650 us
  waiting for transfers between devices  574 us (88%)
  local copies, waits for them, and re-layouts  22.5 us (3%)
  other arithmetic  16 us (2%)
  matrix products  14.1 us (2%)
  between operations  13.5 us (2%)
  starting transfers between devices  10.3 us (2%)
    all_to_all x1, waiting for transfers between devices, shards(): lax.all_to_all(outgoing, 'rows', split_axis=0, concat_axis=0, tiled=True)  426 us
    reduce_scatter x1, waiting for transfers between devices, shards(): lax.psum_scatter(partial_tile, 'rows', scatter_dimension=0, tiled=True)  147 us
    select_n x1, other arithmetic, shards(): jnp.where(filled[:, :, None, None], own_blocks[local_pick], jnp.zeros((),...  14 us
  transfers between devices with their start and end apart: 3, of which 2 were waited for; matrix products, arithmetic and copies ran while one was open for 4% of the time, Pallas kernels for 0%

commit v1 on v0

v1 whole, which is shorter than its diff:
```python
import jax
import jax.numpy as jnp
from jax import lax
from jax.sharding import PartitionSpec as P

BLK = 256


def shards(psi_low, psi_high, dip_blocks, block_cols):
    own_index = lax.axis_index("rows")
    rows_dev, columns = psi_high.shape
    per_dev = dip_blocks.shape[0]
    rb_dev = rows_dev // BLK
    knz = per_dev // rb_dev
    own_list = lax.dynamic_slice_in_dim(block_cols, own_index * per_dev, per_dev)
    low = lax.all_gather(psi_low, "jpair", axis=1, tiled=True)
    high = lax.all_gather(psi_high, "rows", axis=0, tiled=True).reshape(-1, BLK, columns)
    fetched = high[own_list].reshape(rb_dev, knz, BLK, columns)
    dip = dip_blocks.reshape(rb_dev, knz, BLK, BLK)
    applied = jnp.einsum("qkab,qkbc->qac", dip, fetched, preferred_element_type=jnp.float32)
    applied = applied.reshape(rows_dev, columns).astype(jnp.bfloat16)
    partial_tile = jnp.dot(low.T, applied, preferred_element_type=jnp.float32)
    return lax.psum_scatter(partial_tile, "rows", scatter_dimension=0, tiled=True)


def solution(mesh):
    placed = (P("rows", "jpair"), P("rows", "jpair"), P("rows", None, None), P())
    return jax.shard_map(
        shards, mesh=mesh, in_specs=placed, out_specs=P("rows", "jpair"), check_vma=False
    )
```

time: 655 us -> 382 us (0.58)
  waiting for transfers between devices: 574 us -> 338 us
  other arithmetic: 16 us -> 0.77 us
  starting transfers between devices: 10.3 us -> 0.08 us
  local copies, waits for them, and re-layouts: 22.5 us -> 13.2 us
    all_to_all x1 -> x0, waiting for transfers between devices: 426 us -> none  [shards(): lax.all_to_all(outgoing, 'rows', split_axis=0, concat_axis=0, tiled=True)]
    all_gather x1 -> x2, waiting for transfers between devices: 0.02 us -> 198 us  [the longest x1 104 us: shards(): lax.all_gather(psi_high, 'rows', axis=0, tiled=True)]
    select_n x4 -> x1, other arithmetic: 14.8 us -> 0.77 us  [shards(): fetched = high[own_list].reshape(rb_dev, knz, BLK, columns)]
    all_to_all x1 -> x0, starting transfers between devices: 10.2 us -> none  [shards(): lax.all_to_all(outgoing, 'rows', split_axis=0, concat_axis=0, tiled=True)]
    reduce_scatter x1, waiting for transfers between devices: 147 us -> 138 us  [shards(): lax.psum_scatter(partial_tile, 'rows', scatter_dimension=0, tiled=True)]
    gather x2 -> x1, local copies, waits for them, and re-layouts: 19.3 us -> 11.3 us  [shards(): fetched = high[own_list].reshape(rb_dev, knz, BLK, columns)]
  transfers between devices with their start and end apart: 3 -> 3, of which waited for: 2 -> 3; matrix products, arithmetic and copies ran while one was open for 4% -> 5% of each run, Pallas kernels for 0% -> 0%
where the time goes in v1:
time: 382 us; the launch traced here: 377 us
  waiting for transfers between devices  338 us (88%)
  local copies, waits for them, and re-layouts  13.2 us (3%)
  between operations  13.1 us (3%)
  matrix products  12 us (3%)
    reduce_scatter x1, waiting for transfers between devices, shards(): lax.psum_scatter(partial_tile, 'rows', scatter_dimension=0, tiled=True)  138 us
    all_gather x1, waiting for transfers between devices, shards(): lax.all_gather(psi_high, 'rows', axis=0, tiled=True)  104 us
    all_gather x1, waiting for transfers between devices, shards(): low = lax.all_gather(psi_low, 'jpair', axis=1, tiled=True)  93.7 us
    gather x1, local copies, waits for them, and re-layouts, shards(): fetched = high[own_list].reshape(rb_dev, knz, BLK, columns)  11.3 us
    dot_general x1, matrix products, shards(): jnp.einsum('qkab,qkbc->qac', dip, fetched, preferred_element_type=jnp.flo...  8.51 us
  transfers between devices with their start and end apart: 3, of which 3 were waited for; matrix products, arithmetic and copies ran while one was open for 5% of the time, Pallas kernels for 0%

profile of v1, /device:TPU:1, one launch (start us, length us, event | category | flops | bytes accessed | tf_op | source)
XLA Modules:
  0.0 376.9 jit_solution(7286679104696525465)
XLA Ops:
  6.5 0.0 all-gather.3.cloned.1.call-start
  6.5 0.7 all-gather.3.cloned.1.call-update
  7.3 0.0 all-gather.5.cloned.1.call-start
  7.3 0.7 all-gather.5.cloned.1.call-update
  8.0 0.0 reduce-scatter.4.cloned.1.call-start
  8.1 0.8 compare_select_fusion
  8.8 104.4 %all-gather.3.cloned.1.call-done = bf16[32768,256]{1,0:T(8,128)(2,1)} async-done(((bf16[1024,256]{1,0:T(8,128)(2,1)}), bf16[32768,256]{1,0:T(8,128)(2,1)}) %all-gather.3.cloned.1.call-update) | async-done | bytes 16777232 | tf_op jit(solution)/shard_map/all_gather | solution.py:17
  113.2 11.3 %gather_fusion = bf16[64,256,256]{2,1,0:T(8,128)(2,1)} fusion(bf16[128,256,256]{2,1,0:T(8,128)(2,1)} %bitcast.19, s32[1024]{0:T(1024)S(1)} %pad_clamp_fusion), kind=kCustom, calls=%fused_computation | custom fusion | bytes 16777472 | tf_op jit(solution)/shard_map/gather | solution.py:18
  124.5 8.5 %fusion = bf16[4,256,256]{1,2,0:T(8,128)(2,1)S(1)} fusion(bf16[4,16,256,256]{3,2,1,0:T(8,128)(2,1)} %bitcast.20, bf16[4,16,256,256]{3,2,1,0:T(8,128)(2,1)} %bitcast.18), kind=kOutput, calls=%fused_computation.3 | convolution fusion | flops 2147745792 | bytes 17301504 | tf_op jit(solution)/shard_map/qkab,qkbc->qac/dot_general | solution.py:20
  133.0 93.7 %all-gather.5.cloned.1.call-done = bf16[1024,2048]{1,0:T(8,128)(2,1)} async-done(((bf16[1024,256]{1,0:T(8,128)(2,1)}), bf16[1024,2048]{1,0:T(8,128)(2,1)}) %all-gather.5.cloned.1.call-update) | async-done | bytes 4194320 | tf_op jit(solution)/shard_map/all_gather | solution.py:16
  226.7 3.5 convolution_bitcast_fusion
  230.2 1.9 copy.8
  232.1 0.0 reduce-scatter.4.cloned.1.call-update
  232.1 138.3 %reduce-scatter.4.cloned.1.call-done = f32[64,256]{1,0:T(8,128)} async-done(((f32[2048,256]{1,0:T(8,128)}), f32[64,256]{1,0:T(8,128)}) %reduce-scatter.4.cloned.1.call-update) | async-done | bytes 65552 | tf_op jit(solution)/shard_map/reduce_scatter | solution.py:23
  (1 shorter events, 0.0 us)
Async XLA Ops:
  6.5 106.7 %all-gather.3.cloned.1.call-start = ((), (), s32[]{:S(2)}) async-start(), calls=%async_computation.1 | async-start | bytes 17301504 | tf_op jit(solution)/shard_map/all_gather | solution.py:17
  7.3 219.5 %all-gather.5.cloned.1.call-start = ((), (), s32[]{:S(2)}) async-start(), calls=%async_computation.2 | async-start | bytes 4718592 | tf_op jit(solution)/shard_map/all_gather | solution.py:16
  8.0 362.4 %reduce-scatter.4.cloned.1.call-start = ((), (), s32[]{:S(2)}) async-start(), calls=%async_computation.3 | async-start | bytes 2162688 | tf_op jit(solution)/shard_map/reduce_scatter | solution.py:23
Sparse Core Ops, SparseCore 0:
  9.2 103.9 all-gather.2
  115.7 111.0 all-gather.4
  232.2 138.1 reduce-scatter.3

commit v2 on v1

v2 whole, which is shorter than its diff:
```python
import functools

import jax
import jax.numpy as jnp
from jax import lax
from jax.experimental import pallas as pl
from jax.experimental.pallas import tpu as pltpu
from jax.sharding import PartitionSpec as P

BLK = 256
LANES = 128
MESH = pl.DeviceIdType.MESH
RING = 4
Y_TYPE = jnp.bfloat16
Z_TYPE = jnp.bfloat16


def kernel(
    cols, low, high, dip, out,
    g_a, g_b, d_buf, low_buf, low_t, applied, tile_a, tile_b, sib_buf, y_send, y_recv, z_send, z_recv,
    recv_g, send_g, recv_low, send_low, recv_sum, send_sum, local_sem,
):
    gathered = (g_a, g_b)
    tiles = (tile_a, tile_b)
    jp = lax.axis_index("jpair")
    rw = lax.axis_index("rows")
    x, zh = lax.rem(jp, RING), lax.div(jp, RING)
    c, y, z = lax.rem(rw, 2), lax.rem(lax.div(rw, 2), RING), lax.div(rw, 2 * RING)

    def rows_of(zs, ys, cs):
        return (zs * RING + ys) * 2 + cs

    def ring(v, step):
        return lax.rem(v + step + RING, RING)

    def at_rows(zs, ys, cs):
        return (jp, rows_of(zs, ys, cs))

    def at_jpair(zhs, xs):
        return (zhs * RING + xs, rw)

    right, left = at_rows(z, ring(y, 1), c), at_rows(z, ring(y, -1), c)
    sibling = at_rows(z, y, 1 - c)
    y_others = [at_rows(z, ring(y, d), c) for d in (1, 2, 3)]
    z_others = [at_rows(ring(z, d), y, c) for d in (1, 2, 3)]
    x_others = [at_jpair(zh, ring(x, d)) for d in (1, 2, 3)]
    across = at_jpair(1 - zh, x)

    barrier = pltpu.get_barrier_semaphore()
    partners = [sibling, across] + y_others + z_others + x_others
    for partner in partners:
        pl.semaphore_signal(barrier, inc=1, device_id=partner, device_id_type=MESH)
    pl.semaphore_wait(barrier, len(partners))

    last_waits = []

    def remote(src, dst, send_sem, recv_sem, target):
        return pltpu.make_async_remote_copy(
            src_ref=src, dst_ref=dst, send_sem=send_sem, recv_sem=recv_sem,
            device_id=target, device_id_type=MESH,
        )

    counts = [0, 0]

    def piece(h, r, half):
        return gathered[h].at[pl.ds(r * 4 + 2 * half, 2)]

    def send(h, r, half, target, src=None, cond=None):
        slot = counts[h]
        counts[h] += 1
        dst = piece(h, r, half)
        copy = remote(dst if src is None else src, dst, send_g.at[h, slot], recv_g.at[h, r, half], target)
        if cond is None:
            copy.start()
            last_waits.append(copy.wait_send)
        else:
            pl.when(cond)(copy.start)
            last_waits.append(lambda: pl.when(cond)(copy.wait_send))

    def arrive(h, r, half):
        ref = piece(h, r, half)
        remote(ref, ref, send_g.at[h, 0], recv_g.at[h, r, half], sibling).wait_recv()

    def own_part(h, half):
        return high.at[pl.ds(2 * half, 2), :, pl.ds(LANES * h, LANES)]

    up, down = at_rows(lax.rem(z + 1, RING), y, c), at_rows(ring(z, -1), y, c)
    sources = [z, z + 1 - 2 * lax.rem(z, 2), jnp.where(z < 2, 2, 1), jnp.where(z < 2, 3, 0)]

    def own_z(h):
        for half in (0, 1):
            send(h, rw, half, up, own_part(h, half), z < RING - 1)
            send(h, rw, half, down, own_part(h, half), z > 0)

    def own_y(h):
        for half in (0, 1):
            send(h, rw, half, right, own_part(h, half))
            send(h, rw, 1 - half, left, own_part(h, 1 - half))
        for half in (0, 1):
            send(h, rw, half, sibling, own_part(h, half))
        copy = pltpu.make_async_copy(
            high.at[:, :, pl.ds(LANES * h, LANES)], gathered[h].at[pl.ds(rw * 4, 4)], local_sem.at[h]
        )
        copy.start()
        return copy

    def from_z(h, g):
        zs = sources[g]
        r = rows_of(zs, y, c)
        below = zs < z
        onward = jnp.logical_or(jnp.logical_and(below, z < RING - 1), jnp.logical_and(zs > z, z > 0))
        target = at_rows(jnp.where(below, lax.rem(z + 1, RING), ring(z, -1)), y, c)
        for half in (0, 1):
            arrive(h, r, half)
            send(h, r, half, target, cond=onward)
            send(h, r, half, right)
            send(h, r, half, left)
            send(h, r, half, sibling)

    def from_y(h, g):
        r_left = rows_of(sources[g], ring(y, -1), c)
        r_right = rows_of(sources[g], ring(y, 1), c)
        for half in (0, 1):
            arrive(h, r_left, half)
            if half == 0:
                send(h, r_left, half, right)
            send(h, r_left, half, sibling)
            arrive(h, r_right, half)
            if half == 1:
                send(h, r_right, half, left)
            send(h, r_right, half, sibling)

    def from_far(h, g):
        r = rows_of(sources[g], ring(y, 2), c)
        for half in (0, 1):
            arrive(h, r, half)
            send(h, r, half, sibling)

    def from_sibling(h):
        for zs in range(RING):
            for ys in range(RING):
                for half in (0, 1):
                    arrive(h, rows_of(zs, ys, 1 - c), half)

    low_count = [0]

    def send_low_to(j, target, src):
        slot = low_count[0]
        low_count[0] += 1
        copy = remote(src, low_buf.at[j], send_low.at[slot], recv_low.at[j], target)
        copy.start()
        last_waits.append(copy.wait_send)

    def arrive_low(j):
        remote(low_buf.at[j], low_buf.at[j], send_low.at[0], recv_low.at[j], sibling).wait_recv()

    j_across = (1 - zh) * RING + x

    def low_start():
        for target in x_others:
            send_low_to(jp, target, low)

    def low_across():
        send_low_to(jp, across, low)

    def low_onward():
        arrive_low(j_across)
        for target in x_others:
            send_low_to(j_across, target, low_buf.at[j_across])

    def low_finish():
        own_low.wait()
        for d in (1, 2, 3):
            arrive_low(zh * RING + ring(x, d))
        for d in (1, 2, 3):
            arrive_low((1 - zh) * RING + ring(x, d))

    def low_turn(j):
        low_t[pl.ds(j * BLK, BLK), :] = low_buf[j].T

    def apply_rows(h, q):
        def some(i, total):
            for k in range(4):
                b = q * 16 + i * 4 + k
                total = total + jnp.dot(d_buf[b], gathered[h][cols[rw * 64 + b]], preferred_element_type=jnp.float32)
            return total

        total = lax.fori_loop(0, 4, some, jnp.zeros((BLK, LANES), jnp.float32))
        applied[h, pl.ds(q * BLK, BLK), :] = total.astype(jnp.bfloat16)

    def tile_rows(h, j0, n):
        def one(j, _):
            part = jnp.dot(
                low_t[pl.ds(pl.multiple_of(j * BLK, BLK), BLK), :], applied[h], preferred_element_type=jnp.float32
            )
            tiles[h][pl.ds(2 * j, 2)] = part.reshape(2, 2, 64, LANES)
            return 0

        lax.fori_loop(j0, j0 + n, one, 0)

    def sum_copy(h, k, src, dst, target):
        return remote(src, dst, send_sum.at[h, k], recv_sum.at[h, k], target)

    def sum_sibling(h):
        copy = sum_copy(h, 0, tiles[h].at[:, 1 - c], sib_buf.at[h], sibling)
        copy.start()
        return copy

    def sum_y_start(h, sib_copy):
        sib_copy.wait()
        copies = []
        for d in (2, 1, 3):
            for zs in range(RING):
                p = zs * RING + ring(y, d)
                y_send[h, d, zs] = (tiles[h][p, c] + sib_buf[h, p]).astype(Y_TYPE)
            copy = sum_copy(h, d, y_send.at[h, d], y_recv.at[h, d], y_others[d - 1])
            copy.start()
            copies.append(copy)
        return copies

    def sum_z_start(h, y_copies):
        for copy in y_copies:
            copy.wait()

        def one(zs):
            p = zs * RING + y
            total = tiles[h][p, c] + sib_buf[h, p]
            for d in (1, 2, 3):
                total = total + y_recv[h, d, zs].astype(jnp.float32)
            return total

        copies = []
        for d in (3, 2, 1):
            z_send[h, d] = one(ring(z, d)).astype(Z_TYPE)
            copy = sum_copy(h, 3 + d, z_send.at[h, d], z_recv.at[h, d], z_others[d - 1])
            copy.start()
            copies.append(copy)
        return copies, one(z)

    def sum_end(h, copies, total):
        for copy in copies:
            copy.wait()
        for d in (1, 2, 3):
            total = total + z_recv[h, d].astype(jnp.float32)
        out[:, LANES * h : LANES * (h + 1)] = total

    own_z(0)
    local_0 = own_y(0)
    low_start()
    own_low = pltpu.make_async_copy(low, low_buf.at[jp], local_sem.at[2])
    own_low.start()
    dip_copy = pltpu.make_async_copy(dip, d_buf, local_sem.at[3])
    dip_copy.start()

    from_z(0, 1)
    from_y(0, 0)
    from_z(0, 2)
    own_z(1)
    low_across()
    from_far(0, 0)
    from_z(0, 3)
    from_y(0, 1)
    from_far(0, 1)
    local_1 = own_y(1)
    from_y(0, 2)
    from_far(0, 2)
    low_onward()
    from_z(1, 1)
    from_y(0, 3)
    from_far(0, 3)
    from_sibling(0)
    local_0.wait()
    dip_copy.wait()
    from_z(1, 2)
    apply_rows(0, 0)
    from_y(1, 0)
    apply_rows(0, 1)
    from_far(1, 0)
    from_z(1, 3)
    apply_rows(0, 2)
    from_y(1, 1)
    apply_rows(0, 3)
    from_far(1, 1)
    low_finish()
    for j in range(4):
        low_turn(j)
    from_y(1, 2)
    for j in range(4, 8):
        low_turn(j)
    from_far(1, 2)
    tile_rows(0, 0, 4)
    tile_rows(0, 4, 4)
    sib_copy = sum_sibling(0)
    from_y(1, 3)
    y_copies = sum_y_start(0, sib_copy)
    from_far(1, 3)
    z_copies, mine = sum_z_start(0, y_copies)
    from_sibling(1)
    local_1.wait()
    for q in range(4):
        apply_rows(1, q)
    sum_end(0, z_copies, mine)
    tile_rows(1, 0, 8)
    sib_copy = sum_sibling(1)
    y_copies = sum_y_start(1, sib_copy)
    z_copies, mine = sum_z_start(1, y_copies)
    for wait in last_waits:
        wait()
    sum_end(1, z_copies, mine)


def shards(psi_low, psi_high, dip_blocks, block_cols):
    any_space = pl.BlockSpec(memory_space=pl.ANY)
    return pl.pallas_call(
        kernel,
        out_shape=jax.ShapeDtypeStruct((64, 256), jnp.float32),
        in_specs=[pl.BlockSpec(memory_space=pltpu.SMEM), any_space, any_space, any_space],
        out_specs=pl.BlockSpec(memory_space=pltpu.VMEM),
        scratch_shapes=[
            pltpu.VMEM((128, BLK, LANES), jnp.bfloat16),
            pltpu.VMEM((128, BLK, LANES), jnp.bfloat16),
            pltpu.VMEM((64, BLK, BLK), jnp.bfloat16),
            pltpu.VMEM((8, 1024, 256), jnp.bfloat16),
            pltpu.VMEM((2048, 1024), jnp.bfloat16),
            pltpu.VMEM((2, 1024, LANES), jnp.bfloat16),
            pltpu.VMEM((16, 2, 64, LANES), jnp.float32),
            pltpu.VMEM((16, 2, 64, LANES), jnp.float32),
            pltpu.VMEM((2, 16, 64, LANES), jnp.float32),
            pltpu.VMEM((2, 4, 4, 64, LANES), Y_TYPE),
            pltpu.VMEM((2, 4, 4, 64, LANES), Y_TYPE),
            pltpu.VMEM((2, 4, 64, LANES), Z_TYPE),
            pltpu.VMEM((2, 4, 64, LANES), Z_TYPE),
            pltpu.SemaphoreType.DMA((2, 32, 2)),
            pltpu.SemaphoreType.DMA((2, 72)),
            pltpu.SemaphoreType.DMA((8,)),
            pltpu.SemaphoreType.DMA((8,)),
            pltpu.SemaphoreType.DMA((2, 8)),
            pltpu.SemaphoreType.DMA((2, 8)),
            pltpu.SemaphoreType.DMA((4,)),
        ],
        compiler_params=pltpu.CompilerParams(
            collective_id=0, has_side_effects=True, vmem_limit_bytes=56 * 1024 * 1024
        ),
        cost_estimate=pl.CostEstimate(flops=3 * 2**30, bytes_accessed=10 * 2**20, transcendentals=0),
    )(block_cols, psi_low, psi_high.reshape(4, BLK, 256), dip_blocks)


def solution(mesh):
    placed = (P("rows", "jpair"), P("rows", "jpair"), P("rows", None, None), P())
    return jax.shard_map(
        shards, mesh=mesh, in_specs=placed, out_specs=P("rows", "jpair"), check_vma=False
    )
```

time: 382 us -> 143 us (0.37); the launches traced: 377 us -> 143 us
  waiting for transfers between devices: 338 us -> 0 us
  Pallas kernels: 0 us -> 141 us
  between operations: 13.1 us -> 0.01 us
  matrix products: 12 us -> 0 us
  local copies, waits for them, and re-layouts: 13.2 us -> 1.47 us
    all_gather x2 -> x0, waiting for transfers between devices: 198 us -> none  [the longest x1 104 us: shards(): lax.all_gather(psi_high, 'rows', axis=0, tiled=True)]
    pallas_call x0 -> x1, Pallas kernels: none -> 141 us  [shards(): pl.pallas_call(kernel, out_shape=jax.ShapeDtypeStruct((64, 256), jnp.floa...]
    reduce_scatter x1 -> x0, waiting for transfers between devices: 138 us -> none  [shards(): lax.psum_scatter(partial_tile, 'rows', scatter_dimension=0, tiled=True)]
    dot_general x2 -> x0, matrix products: 12 us -> none  [the longest x1 8.51 us: shards(): jnp.einsum('qkab,qkbc->qac', dip, fetched, preferred_element_type=jnp.flo...]
    gather x1 -> x0, local copies, waits for them, and re-layouts: 11.3 us -> none  [shards(): fetched = high[own_list].reshape(rb_dev, knz, BLK, columns)]
  transfers between devices with their start and end apart: 3 -> 0, of which waited for: 3 -> 0; matrix products, arithmetic and copies ran while one was open for 5% -> 0% of each run, Pallas kernels for 0% -> 0%
where the time goes in v2:
time: 143 us
  Pallas kernels  141 us (99%)
  local copies, waits for them, and re-layouts  1.47 us (1%)
    pallas_call x1, Pallas kernels, shards(): pl.pallas_call(kernel, out_shape=jax.ShapeDtypeStruct((64, 256), jnp.floa...  141 us

profile of v2, /device:TPU:1, one launch (start us, length us, event | category | flops | bytes accessed | tf_op | source)
XLA Modules:
  0.0 142.7 jit_solution(14984865731934130835)
XLA Ops:
  0.0 141.3 %shard_map.46 = f32[64,256]{1,0:T(8,128)} custom-call(s32[2048]{0:T(1024)} %cols.1, bf16[1024,256]{1,0:T(8,128)(2,1)} %low.1, bf16[4,256,256]{2,1,0:T(8,128)(2,1)} %bitcast.1, bf16[64,256,256]{2,1,0:T(8,128)(2,1)} %dip.1), custom_call_target="tpu_custom_call" | custom-call | flops 3221225472 | bytes 10485760 | tf_op jit(solution)/shard_map/pallas_call | solution.py:314
  141.3 1.5 %copy.6 = f32[64,256]{1,0:T(8,128)} copy(f32[64,256]{1,0:T(8,128)} %shard_map.46) | data formatting | bytes 131072

commit v3 on v2

--- a/solution.py
+++ b/solution.py
@@ -52,7 +52,7 @@
         pl.semaphore_signal(barrier, inc=1, device_id=partner, device_id_type=MESH)
     pl.semaphore_wait(barrier, len(partners))
 
-    last_waits = []
+    waits = {}
 
     def remote(src, dst, send_sem, recv_sem, target):
         return pltpu.make_async_remote_copy(
@@ -60,120 +60,135 @@
             device_id=target, device_id_type=MESH,
         )
 
-    counts = [0, 0]
-
-    def piece(h, r, half):
-        return gathered[h].at[pl.ds(r * 4 + 2 * half, 2)]
-
-    def send(h, r, half, target, src=None, cond=None):
-        slot = counts[h]
-        counts[h] += 1
-        dst = piece(h, r, half)
-        copy = remote(dst if src is None else src, dst, send_g.at[h, slot], recv_g.at[h, r, half], target)
-        if cond is None:
-            copy.start()
-            last_waits.append(copy.wait_send)
-        else:
-            pl.when(cond)(copy.start)
-            last_waits.append(lambda: pl.when(cond)(copy.wait_send))
-
-    def arrive(h, r, half):
-        ref = piece(h, r, half)
+    inner = jnp.logical_and(z > 0, z < RING - 1)
+    slots = {}
+
+    def piece(h, r, half, n=1):
+        return gathered[h].at[pl.ds(r * 4 + 2 * half, 2 * n)]
+
+    def send(key, h, r, half, target, src=None, n=1, cond=None):
+        dst = piece(h, r, half, n)
+        sem = send_g.at[h, slots.setdefault((h, key), sum(k[0] == h for k in slots))]
+        copy = remote(dst if src is None else src, dst, sem, recv_g.at[h, r, half], target)
+        copy.start()
+        waits[(h, key)] = (n, cond)
+
+    def arrive(h, r, half, n=1):
+        ref = piece(h, r, half, n)
         remote(ref, ref, send_g.at[h, 0], recv_g.at[h, r, half], sibling).wait_recv()
 
-    def own_part(h, half):
-        return high.at[pl.ds(2 * half, 2), :, pl.ds(LANES * h, LANES)]
-
-    up, down = at_rows(lax.rem(z + 1, RING), y, c), at_rows(ring(z, -1), y, c)
+    def own_part(h, half, n=1):
+        return high.at[pl.ds(2 * half, 2 * n), :, pl.ds(LANES * h, LANES)]
+
+    onward = at_rows(jnp.where(z == RING - 1, z - 1, z + 1), y, c)
+    downward = at_rows(ring(z, -1), y, c)
     sources = [z, z + 1 - 2 * lax.rem(z, 2), jnp.where(z < 2, 2, 1), jnp.where(z < 2, 3, 0)]
 
-    def own_z(h):
+    def own_z(h, is_inner):
         for half in (0, 1):
-            send(h, rw, half, up, own_part(h, half), z < RING - 1)
-            send(h, rw, half, down, own_part(h, half), z > 0)
-
-    def own_y(h):
+            send(("own_z", half, 0), h, rw, half, onward, own_part(h, half))
+            if is_inner:
+                send(("own_z", half, 1), h, rw, half, downward, own_part(h, half), cond=inner)
+
+    def own_y(h, is_inner):
         for half in (0, 1):
-            send(h, rw, half, right, own_part(h, half))
-            send(h, rw, 1 - half, left, own_part(h, 1 - half))
+            send(("own_y", half, 0), h, rw, half, right, own_part(h, half))
+            send(("own_y", 1 - half, 1), h, rw, 1 - half, left, own_part(h, 1 - half))
+        send(("own_s",), h, rw, 0, sibling, own_part(h, 0, 2), n=2)
+
+    def from_z(h, g, is_inner, halves=(0, 1)):
+        zs = sources[g]
+        r = rows_of(zs, y, c)
+        target = at_rows(jnp.where(zs < z, lax.rem(z + 1, RING), ring(z, -1)), y, c)
+        for half in halves:
+            arrive(h, r, half)
+            if is_inner:
+                send(("z_z", g, half), h, r, half, target, cond=inner)
+            send(("z_y", g, half, 0), h, r, half, right)
+            send(("z_y", g, half, 1), h, r, half, left)
+        if 1 in halves:
+            send(("z_s", g), h, r, 0, sibling, n=2)
+
+    def from_two(h, g, is_inner):
         for half in (0, 1):
-            send(h, rw, half, sibling, own_part(h, half))
+            from_z(h, g, is_inner, (half,))
+            from_z(h, g + 1, is_inner, (half,))
+
+    def from_y(h, g, is_inner):
+        r_left = rows_of(sources[g], ring(y, -1), c)
+        r_right = rows_of(sources[g], ring(y, 1), c)
+        arrive(h, r_left, 0)
+        send(("y_y", g, 0), h, r_left, 0, right)
+        arrive(h, r_right, 1)
+        send(("y_y", g, 1), h, r_right, 1, left)
+        arrive(h, r_left, 1)
+        send(("y_s", g, 0), h, r_left, 0, sibling, n=2)
+        arrive(h, r_right, 0)
+        send(("y_s", g, 1), h, r_right, 0, sibling, n=2)
+
+    def from_far(h, g, is_inner):
+        r = rows_of(sources[g], ring(y, 2), c)
+        for half in (0, 1):
+            arrive(h, r, half)
+        send(("f_s", g), h, r, 0, sibling, n=2)
+
+    def from_sibling(h):
+        for zs in range(RING):
+            for ys in range(RING):
+                arrive(h, rows_of(zs, ys, 1 - c), 0, 2)
+
+    def local_part(h):
         copy = pltpu.make_async_copy(
             high.at[:, :, pl.ds(LANES * h, LANES)], gathered[h].at[pl.ds(rw * 4, 4)], local_sem.at[h]
         )
         copy.start()
         return copy
 
-    def from_z(h, g):
-        zs = sources[g]
-        r = rows_of(zs, y, c)
-        below = zs < z
-        onward = jnp.logical_or(jnp.logical_and(below, z < RING - 1), jnp.logical_and(zs > z, z > 0))
-        target = at_rows(jnp.where(below, lax.rem(z + 1, RING), ring(z, -1)), y, c)
-        for half in (0, 1):
-            arrive(h, r, half)
-            send(h, r, half, target, cond=onward)
-            send(h, r, half, right)
-            send(h, r, half, left)
-            send(h, r, half, sibling)
-
-    def from_y(h, g):
-        r_left = rows_of(sources[g], ring(y, -1), c)
-        r_right = rows_of(sources[g], ring(y, 1), c)
-        for half in (0, 1):
-            arrive(h, r_left, half)
-            if half == 0:
-                send(h, r_left, half, right)
-            send(h, r_left, half, sibling)
-            arrive(h, r_right, half)
-            if half == 1:
-                send(h, r_right, half, left)
-            send(h, r_right, half, sibling)
-
-    def from_far(h, g):
-        r = rows_of(sources[g], ring(y, 2), c)
-        for half in (0, 1):
-            arrive(h, r, half)
-            send(h, r, half, sibling)
-
-    def from_sibling(h):
-        for zs in range(RING):
-            for ys in range(RING):
-                for half in (0, 1):
-                    arrive(h, rows_of(zs, ys, 1 - c), half)
-
-    low_count = [0]
-
-    def send_low_to(j, target, src):
-        slot = low_count[0]
-        low_count[0] += 1
-        copy = remote(src, low_buf.at[j], send_low.at[slot], recv_low.at[j], target)
+    def by_place(inner_steps, end_steps):
+        for is_inner, steps in ((True, inner_steps), (False, end_steps)):
+
+            @pl.when(inner if is_inner else jnp.logical_not(inner))
+            def _(is_inner=is_inner, steps=steps):
+                for step in steps:
+                    step[0](*step[1:], is_inner)
+
+    LOW_PARTS = 4
+
+    def send_low_to(key, j, target, src, part):
+        dst = low_buf.at[j, pl.ds(part * 256, 256)]
+        if src is None:
+            src = dst
+        sem = send_low.at[slots.setdefault(("low", key), sum(k[0] == "low" for k in slots))]
+        copy = remote(src, dst, sem, recv_low.at[j, part], target)
         copy.start()
-        last_waits.append(copy.wait_send)
-
-    def arrive_low(j):
-        remote(low_buf.at[j], low_buf.at[j], send_low.at[0], recv_low.at[j], sibling).wait_recv()
+        waits[("low", key)] = (0, None)
+
+    def arrive_low(j, part):
+        dst = low_buf.at[j, pl.ds(part * 256, 256)]
+        remote(dst, dst, send_low.at[0], recv_low.at[j, part], sibling).wait_recv()
 
     j_across = (1 - zh) * RING + x
 
-    def low_start():
-        for target in x_others:
-            send_low_to(jp, target, low)
-
-    def low_across():
-        send_low_to(jp, across, low)
-
-    def low_onward():
-        arrive_low(j_across)
-        for target in x_others:
-            send_low_to(j_across, target, low_buf.at[j_across])
+    def low_x(is_inner):
+        for part in range(LOW_PARTS):
+            for d in range(3):
+                send_low_to(("x", d, part), jp, x_others[d], low.at[pl.ds(part * 256, 256)], part)
+
+    def low_across(part, is_inner):
+        send_low_to(("across", part), jp, across, low.at[pl.ds(part * 256, 256)], part)
+
+    def low_onward(part, is_inner):
+        arrive_low(j_across, part)
+        for d in range(3):
+            send_low_to(("onward", d, part), j_across, x_others[d], None, part)
 
     def low_finish():
         own_low.wait()
-        for d in (1, 2, 3):
-            arrive_low(zh * RING + ring(x, d))
-        for d in (1, 2, 3):
-            arrive_low((1 - zh) * RING + ring(x, d))
+        for part in range(LOW_PARTS):
+            for d in (1, 2, 3):
+                arrive_low(zh * RING + ring(x, d), part)
+            for d in (1, 2, 3):
+                arrive_low((1 - zh) * RING + ring(x, d), part)
 
     def low_turn(j):
         low_t[pl.ds(j * BLK, BLK), :] = low_buf[j].T
@@ -244,68 +259,69 @@
             total = total + z_recv[h, d].astype(jnp.float32)
         out[:, LANES * h : LANES * (h + 1)] = total
 
-    own_z(0)
-    local_0 = own_y(0)
-    low_start()
+    by_place([(own_z, 0), (own_y, 0)], [(own_z, 0), (own_y, 0)])
+    local_0 = local_part(0)
     own_low = pltpu.make_async_copy(low, low_buf.at[jp], local_sem.at[2])
     own_low.start()
     dip_copy = pltpu.make_async_copy(dip, d_buf, local_sem.at[3])
     dip_copy.start()
-
-    from_z(0, 1)
-    from_y(0, 0)
-    from_z(0, 2)
-    own_z(1)
-    low_across()
-    from_far(0, 0)
-    from_z(0, 3)
-    from_y(0, 1)
-    from_far(0, 1)
-    local_1 = own_y(1)
-    from_y(0, 2)
-    from_far(0, 2)
-    low_onward()
-    from_z(1, 1)
-    from_y(0, 3)
-    from_far(0, 3)
+    low_x(None)
+    local_1 = local_part(1)
+    by_place(
+        [(from_two, 0, 1), (from_y, 0, 0), (from_z, 0, 3), (low_across, 0), (low_across, 1), (from_y, 0, 1), (from_far, 0, 0),
+         (from_y, 0, 2), (own_y, 1), (own_z, 1), (low_across, 2), (from_far, 0, 1), (from_y, 0, 3), (from_far, 0, 2), (from_two, 1, 1), (from_far, 0, 3)],
+        [(from_z, 0, 1), (from_y, 0, 0), (from_y, 0, 1), (from_z, 0, 2), (from_far, 0, 0), (from_z, 0, 3), (low_across, 0), (low_across, 1),
+         (from_y, 0, 2), (from_far, 0, 1), (own_y, 1), (own_z, 1), (low_across, 2), (from_y, 0, 3), (from_far, 0, 2), (from_z, 1, 1), (from_far, 0, 3)],
+    )
     from_sibling(0)
     local_0.wait()
     dip_copy.wait()
-    from_z(1, 2)
+    by_place([(from_y, 1, 0), (from_z, 1, 3), (low_across, 3)], [(from_y, 1, 0), (from_z, 1, 2), (low_across, 3)])
     apply_rows(0, 0)
-    from_y(1, 0)
+    low_onward(0, None)
+    low_onward(1, None)
+    by_place([(from_y, 1, 1)], [(from_y, 1, 1)])
     apply_rows(0, 1)
-    from_far(1, 0)
-    from_z(1, 3)
+    by_place([], [(from_z, 1, 3)])
     apply_rows(0, 2)
-    from_y(1, 1)
+    by_place([(from_far, 1, 0)], [(from_far, 1, 0)])
+    low_onward(2, None)
     apply_rows(0, 3)
-    from_far(1, 1)
+    by_place([(from_y, 1, 2)], [(from_y, 1, 2)])
+    low_onward(3, None)
+    by_place([(from_far, 1, 1)], [(from_far, 1, 1)])
+    by_place([(from_y, 1, 3)], [(from_y, 1, 3)])
     low_finish()
-    for j in range(4):
+    for j in range(8):
         low_turn(j)
-    from_y(1, 2)
-    for j in range(4, 8):
-        low_turn(j)
-    from_far(1, 2)
-    tile_rows(0, 0, 4)
-    tile_rows(0, 4, 4)
+    by_place([(from_far, 1, 2)], [(from_far, 1, 2)])
+    tile_rows(0, 0, 8)
     sib_copy = sum_sibling(0)
-    from_y(1, 3)
+    by_place([(from_far, 1, 3)], [(from_far, 1, 3)])
     y_copies = sum_y_start(0, sib_copy)
-    from_far(1, 3)
-    z_copies, mine = sum_z_start(0, y_copies)
     from_sibling(1)
     local_1.wait()
-    for q in range(4):
+    apply_rows(1, 0)
+    z_copies, mine = sum_z_start(0, y_copies)
+    for q in range(1, 4):
         apply_rows(1, q)
     sum_end(0, z_copies, mine)
     tile_rows(1, 0, 8)
     sib_copy = sum_sibling(1)
     y_copies = sum_y_start(1, sib_copy)
     z_copies, mine = sum_z_start(1, y_copies)
-    for wait in last_waits:
-        wait()
+    for (h, key), (n, cond) in waits.items():
+        slot = slots[(h, key)]
+        if h == "low":
+            ref = low_buf.at[0, pl.ds(0, 256)]
+            copy = remote(ref, ref, send_low.at[slot], recv_low.at[0, 0], sibling)
+        else:
+            ref = gathered[h].at[pl.ds(0, 2 * n)]
+            copy = remote(ref, ref, send_g.at[h, slot], recv_g.at[h, 0, 0], sibling)
+        if cond is None:
+            copy.wait_send()
+        else:
+            pl.when(cond)(copy.wait_send)
     sum_end(1, z_copies, mine)
 
 
@@ -332,8 +348,8 @@
             pltpu.VMEM((2, 4, 64, LANES), Z_TYPE),
             pltpu.SemaphoreType.DMA((2, 32, 2)),
             pltpu.SemaphoreType.DMA((2, 72)),
-            pltpu.SemaphoreType.DMA((8,)),
-            pltpu.SemaphoreType.DMA((8,)),
+            pltpu.SemaphoreType.DMA((8, 4)),
+            pltpu.SemaphoreType.DMA((32,)),
             pltpu.SemaphoreType.DMA((2, 8)),
             pltpu.SemaphoreType.DMA((2, 8)),
             pltpu.SemaphoreType.DMA((4,)),

time: 143 us -> 117 us (0.82)
  Pallas kernels: 141 us -> 115 us
    pallas_call x1, Pallas kernels: 141 us -> 115 us  [shards(): pl.pallas_call(kernel, out_shape=jax.ShapeDtypeStruct((64, 256), jnp.floa...]
where the time goes in v3:
time: 117 us
  Pallas kernels  115 us (98%)
  local copies, waits for them, and re-layouts  1.47 us (1%)
    pallas_call x1, Pallas kernels, shards(): pl.pallas_call(kernel, out_shape=jax.ShapeDtypeStruct((64, 256), jnp.floa...  115 us

profile of v3, /device:TPU:1, one launch (start us, length us, event | category | flops | bytes accessed | tf_op | source)
XLA Modules:
  0.0 116.5 jit_solution(3444034008630420624)
XLA Ops:
  0.0 115.1 %shard_map.46 = f32[64,256]{1,0:T(8,128)} custom-call(s32[2048]{0:T(1024)} %cols.1, bf16[1024,256]{1,0:T(8,128)(2,1)} %low.1, bf16[4,256,256]{2,1,0:T(8,128)(2,1)} %bitcast.1, bf16[64,256,256]{2,1,0:T(8,128)(2,1)} %dip.1), custom_call_target="tpu_custom_call" | custom-call | flops 3221225472 | bytes 10485760 | tf_op jit(solution)/shard_map/pallas_call | solution.py:330
  115.1 1.5 %copy.6 = f32[64,256]{1,0:T(8,128)} copy(f32[64,256]{1,0:T(8,128)} %shard_map.46) | data formatting | bytes 131072

commit v4 on v3

--- a/solution.py
+++ b/solution.py
@@ -11,14 +11,15 @@
 LANES = 128
 MESH = pl.DeviceIdType.MESH
 RING = 4
+GROUP = 4
 Y_TYPE = jnp.bfloat16
 Z_TYPE = jnp.bfloat16
 
 
 def kernel(
-    cols, low, high, dip, out,
+    cols_all, low, high, dip, out,
     g_a, g_b, d_buf, low_buf, low_t, applied, tile_a, tile_b, sib_buf, y_send, y_recv, z_send, z_recv,
-    recv_g, send_g, recv_low, send_low, recv_sum, send_sum, local_sem,
+    recv_g, send_g, recv_low, send_low, recv_sum, send_sum, local_sem, cols,
 ):
     gathered = (g_a, g_b)
     tiles = (tile_a, tile_b)
@@ -195,121 +196,119 @@
 
     def apply_rows(h, q):
         def some(i, total):
-            for k in range(4):
-                b = q * 16 + i * 4 + k
-                total = total + jnp.dot(d_buf[b], gathered[h][cols[rw * 64 + b]], preferred_element_type=jnp.float32)
-            return total
-
-        total = lax.fori_loop(0, 4, some, jnp.zeros((BLK, LANES), jnp.float32))
+            b = q * 16 + i * GROUP
+            lhs = jnp.concatenate([d_buf[b + k] for k in range(GROUP)], axis=1)
+            rhs = jnp.concatenate([gathered[h][cols[rw * 64 + b + k]] for k in range(GROUP)], axis=0)
+            return total + jnp.dot(lhs, rhs, preferred_element_type=jnp.float32)
+
+        total = lax.fori_loop(0, 16 // GROUP, some, jnp.zeros((BLK, LANES), jnp.float32))
         applied[h, pl.ds(q * BLK, BLK), :] = total.astype(jnp.bfloat16)
 
-    def tile_rows(h, j0, n):
-        def one(j, _):
-            part = jnp.dot(
-                low_t[pl.ds(pl.multiple_of(j * BLK, BLK), BLK), :], applied[h], preferred_element_type=jnp.float32
-            )
-            tiles[h][pl.ds(2 * j, 2)] = part.reshape(2, 2, 64, LANES)
-            return 0
-
-        lax.fori_loop(j0, j0 + n, one, 0)
+    quarters = [ring(z, d) for d in (2, 3, 1, 0)]
+    quarter_shift = (2, 3, 1)
 
     def sum_copy(h, k, src, dst, target):
         return remote(src, dst, send_sum.at[h, k], recv_sum.at[h, k], target)
 
-    def sum_sibling(h):
-        copy = sum_copy(h, 0, tiles[h].at[:, 1 - c], sib_buf.at[h], sibling)
-        copy.start()
-        return copy
-
-    def sum_y_start(h, sib_copy):
-        sib_copy.wait()
-        copies = []
+    def sib_copy(h, i):
+        part = pl.ds(4 * quarters[i], 4)
+        return sum_copy(h, i, tiles[h].at[part, 1 - c], sib_buf.at[h, part], sibling)
+
+    def y_copy(h, i, d):
+        return sum_copy(h, 3 + 3 * i + d, y_send.at[h, d, i], y_recv.at[h, d, i], y_others[d - 1])
+
+    def z_copy(h, i):
+        return sum_copy(h, 16 + i, z_send.at[h, i], z_recv.at[h, i], z_others[quarter_shift[i] - 1])
+
+    def tile_quarter(h, i):
+        rows = pl.ds(pl.multiple_of(quarters[i] * 512, 512), 512)
+        part = jnp.dot(low_t[rows, :], applied[h], preferred_element_type=jnp.float32)
+        tiles[h][pl.ds(4 * quarters[i], 4)] = part.reshape(4, 2, 64, LANES)
+        sib_copy(h, i).start()
+
+    def y_quarter(h, i):
+        sib_copy(h, i).wait()
         for d in (2, 1, 3):
-            for zs in range(RING):
-                p = zs * RING + ring(y, d)
-                y_send[h, d, zs] = (tiles[h][p, c] + sib_buf[h, p]).astype(Y_TYPE)
-            copy = sum_copy(h, d, y_send.at[h, d], y_recv.at[h, d], y_others[d - 1])
-            copy.start()
-            copies.append(copy)
-        return copies
-
-    def sum_z_start(h, y_copies):
-        for copy in y_copies:
-            copy.wait()
-
-        def one(zs):
-            p = zs * RING + y
-            total = tiles[h][p, c] + sib_buf[h, p]
-            for d in (1, 2, 3):
-                total = total + y_recv[h, d, zs].astype(jnp.float32)
+            p = quarters[i] * 4 + ring(y, d)
+            y_send[h, d, i] = (tiles[h][p, c] + sib_buf[h, p]).astype(Y_TYPE)
+            y_copy(h, i, d).start()
+
+    def z_quarter(h, i):
+        for d in (1, 2, 3):
+            y_copy(h, i, d).wait()
+        p = quarters[i] * 4 + y
+        total = tiles[h][p, c] + sib_buf[h, p]
+        for d in (1, 2, 3):
+            total = total + y_recv[h, d, i].astype(jnp.float32)
+        if i == 3:
             return total
-
-        copies = []
-        for d in (3, 2, 1):
-            z_send[h, d] = one(ring(z, d)).astype(Z_TYPE)
-            copy = sum_copy(h, 3 + d, z_send.at[h, d], z_recv.at[h, d], z_others[d - 1])
-            copy.start()
-            copies.append(copy)
-        return copies, one(z)
-
-    def sum_end(h, copies, total):
-        for copy in copies:
-            copy.wait()
-        for d in (1, 2, 3):
-            total = total + z_recv[h, d].astype(jnp.float32)
+        z_send[h, i] = total.astype(Z_TYPE)
+        z_copy(h, i).start()
+
+    def sum_end(h, total):
+        for i in range(3):
+            z_copy(h, i).wait()
+            total = total + z_recv[h, i].astype(jnp.float32)
         out[:, LANES * h : LANES * (h + 1)] = total
 
     by_place([(own_z, 0), (own_y, 0)], [(own_z, 0), (own_y, 0)])
     local_0 = local_part(0)
+    low_x(None)
     own_low = pltpu.make_async_copy(low, low_buf.at[jp], local_sem.at[2])
     own_low.start()
     dip_copy = pltpu.make_async_copy(dip, d_buf, local_sem.at[3])
     dip_copy.start()
-    low_x(None)
+    cols_copy = pltpu.make_async_copy(cols_all, cols, local_sem.at[4])
+    cols_copy.start()
     local_1 = local_part(1)
     by_place(
-        [(from_two, 0, 1), (from_y, 0, 0), (from_z, 0, 3), (low_across, 0), (low_across, 1), (from_y, 0, 1), (from_far, 0, 0),
-         (from_y, 0, 2), (own_y, 1), (own_z, 1), (low_across, 2), (from_far, 0, 1), (from_y, 0, 3), (from_far, 0, 2), (from_two, 1, 1), (from_far, 0, 3)],
-        [(from_z, 0, 1), (from_y, 0, 0), (from_y, 0, 1), (from_z, 0, 2), (from_far, 0, 0), (from_z, 0, 3), (low_across, 0), (low_across, 1),
-         (from_y, 0, 2), (from_far, 0, 1), (own_y, 1), (own_z, 1), (low_across, 2), (from_y, 0, 3), (from_far, 0, 2), (from_z, 1, 1), (from_far, 0, 3)],
+        [(from_two, 0, 1), (low_across, 0), (from_y, 0, 0), (from_z, 0, 3), (low_across, 1), (low_across, 2), (from_y, 0, 1), (from_far, 0, 0),
+         (from_y, 0, 2), (own_y, 1), (own_z, 1), (low_onward, 0), (from_far, 0, 1), (from_y, 0, 3), (low_onward, 1), (from_far, 0, 2), (from_two, 1, 1), (from_far, 0, 3)],
+        [(from_z, 0, 1), (from_y, 0, 0), (from_y, 0, 1), (from_z, 0, 2), (low_across, 0), (from_far, 0, 0), (from_z, 0, 3), (low_across, 1), (low_across, 2),
+         (from_y, 0, 2), (from_far, 0, 1), (own_y, 1), (own_z, 1), (low_onward, 0), (from_y, 0, 3), (low_onward, 1), (from_far, 0, 2), (from_z, 1, 1), (from_far, 0, 3)],
     )
     from_sibling(0)
     local_0.wait()
     dip_copy.wait()
-    by_place([(from_y, 1, 0), (from_z, 1, 3), (low_across, 3)], [(from_y, 1, 0), (from_z, 1, 2), (low_across, 3)])
+    cols_copy.wait()
+    by_place([(from_y, 1, 0), (low_across, 3), (low_onward, 2), (from_z, 1, 3)], [(from_y, 1, 0), (low_onward, 2), (from_z, 1, 2), (low_across, 3)])
     apply_rows(0, 0)
-    low_onward(0, None)
-    low_onward(1, None)
+    apply_rows(0, 1)
     by_place([(from_y, 1, 1)], [(from_y, 1, 1)])
-    apply_rows(0, 1)
-    by_place([], [(from_z, 1, 3)])
     apply_rows(0, 2)
-    by_place([(from_far, 1, 0)], [(from_far, 1, 0)])
-    low_onward(2, None)
     apply_rows(0, 3)
+    by_place([(from_far, 1, 0)], [(from_z, 1, 3), (from_far, 1, 0)])
+    low_onward(3, None)
     by_place([(from_y, 1, 2)], [(from_y, 1, 2)])
-    low_onward(3, None)
-    by_place([(from_far, 1, 1)], [(from_far, 1, 1)])
-    by_place([(from_y, 1, 3)], [(from_y, 1, 3)])
     low_finish()
     for j in range(8):
         low_turn(j)
+    for i in range(4):
+        tile_quarter(0, i)
+    by_place([(from_far, 1, 1)], [(from_far, 1, 1)])
+    for i in range(4):
+        y_quarter(0, i)
+    by_place([(from_y, 1, 3)], [(from_y, 1, 3)])
     by_place([(from_far, 1, 2)], [(from_far, 1, 2)])
-    tile_rows(0, 0, 8)
-    sib_copy = sum_sibling(0)
+    mine_0 = [z_quarter(0, i) for i in range(4)][3]
     by_place([(from_far, 1, 3)], [(from_far, 1, 3)])
-    y_copies = sum_y_start(0, sib_copy)
     from_sibling(1)
     local_1.wait()
-    apply_rows(1, 0)
-    z_copies, mine = sum_z_start(0, y_copies)
-    for q in range(1, 4):
+    for q in range(4):
         apply_rows(1, q)
-    sum_end(0, z_copies, mine)
-    tile_rows(1, 0, 8)
-    sib_copy = sum_sibling(1)
-    y_copies = sum_y_start(1, sib_copy)
-    z_copies, mine = sum_z_start(1, y_copies)
+    tile_quarter(1, 0)
+    tile_quarter(1, 1)
+    y_quarter(1, 0)
+    tile_quarter(1, 2)
+    y_quarter(1, 1)
+    tile_quarter(1, 3)
+    y_quarter(1, 2)
+    y_quarter(1, 3)
+    sum_end(0, mine_0)
+    z_quarter(1, 0)
+    z_quarter(1, 1)
+    z_quarter(1, 2)
+    mine_1 = z_quarter(1, 3)
     for (h, key), (n, cond) in waits.items():
         slot = slots[(h, key)]
         if h == "low":
@@ -322,7 +321,7 @@
             copy.wait_send()
         else:
             pl.when(cond)(copy.wait_send)
-    sum_end(1, z_copies, mine)
+    sum_end(1, mine_1)
 
 
 def shards(psi_low, psi_high, dip_blocks, block_cols):
@@ -330,7 +329,7 @@
     return pl.pallas_call(
         kernel,
         out_shape=jax.ShapeDtypeStruct((64, 256), jnp.float32),
-        in_specs=[pl.BlockSpec(memory_space=pltpu.SMEM), any_space, any_space, any_space],
+        in_specs=[any_space] * 4,
         out_specs=pl.BlockSpec(memory_space=pltpu.VMEM),
         scratch_shapes=[
             pltpu.VMEM((128, BLK, LANES), jnp.bfloat16),
@@ -350,9 +349,10 @@
             pltpu.SemaphoreType.DMA((2, 72)),
             pltpu.SemaphoreType.DMA((8, 4)),
             pltpu.SemaphoreType.DMA((32,)),
-            pltpu.SemaphoreType.DMA((2, 8)),
-            pltpu.SemaphoreType.DMA((2, 8)),
-            pltpu.SemaphoreType.DMA((4,)),
+            pltpu.SemaphoreType.DMA((2, 20)),
+            pltpu.SemaphoreType.DMA((2, 20)),
+            pltpu.SemaphoreType.DMA((5,)),
+            pltpu.SMEM((2048,), jnp.int32),
         ],
         compiler_params=pltpu.CompilerParams(
             collective_id=0, has_side_effects=True, vmem_limit_bytes=56 * 1024 * 1024

time: 117 us -> 109 us (0.932)
  Pallas kernels: 115 us -> 107 us
    pallas_call x1, Pallas kernels: 115 us -> 107 us  [shards(): pl.pallas_call(kernel, out_shape=jax.ShapeDtypeStruct((64, 256), jnp.floa...]
where the time goes in v4:
time: 109 us
  Pallas kernels  107 us (98%)
  local copies, waits for them, and re-layouts  1.47 us (1%)
    pallas_call x1, Pallas kernels, shards(): pl.pallas_call(kernel, out_shape=jax.ShapeDtypeStruct((64, 256), jnp.floa...  107 us

profile of v4, /device:TPU:1, one launch (start us, length us, event | category | flops | bytes accessed | tf_op | source)
XLA Modules:
  0.0 108.7 jit_solution(2551380366323164225)
XLA Ops:
  0.0 107.2 %shard_map.46 = f32[64,256]{1,0:T(8,128)} custom-call(s32[2048]{0:T(1024)} %cols_all.1, bf16[1024,256]{1,0:T(8,128)(2,1)} %low.1, bf16[4,256,256]{2,1,0:T(8,128)(2,1)} %bitcast.1, bf16[64,256,256]{2,1,0:T(8,128)(2,1)} %dip.1), custom_call_target="tpu_custom_call" | custom-call | flops 3221225472 | bytes 10485760 | tf_op jit(solution)/shard_map/pallas_call | solution.py:329
  107.2 1.5 %copy.6 = f32[64,256]{1,0:T(8,128)} copy(f32[64,256]{1,0:T(8,128)} %shard_map.46) | data formatting | bytes 131072

commit v5 on v4

--- a/solution.py
+++ b/solution.py
@@ -12,6 +12,7 @@
 MESH = pl.DeviceIdType.MESH
 RING = 4
 GROUP = 4
+LATE = 16
 Y_TYPE = jnp.bfloat16
 Z_TYPE = jnp.bfloat16
 
@@ -20,6 +21,7 @@
     cols_all, low, high, dip, out,
     g_a, g_b, d_buf, low_buf, low_t, applied, tile_a, tile_b, sib_buf, y_send, y_recv, z_send, z_recv,
     recv_g, send_g, recv_low, send_low, recv_sum, send_sum, local_sem, cols,
+    g_late, early, late_parts, late_list,
 ):
     gathered = (g_a, g_b)
     tiles = (tile_a, tile_b)
@@ -48,7 +50,7 @@
     across = at_jpair(1 - zh, x)
 
     barrier = pltpu.get_barrier_semaphore()
-    partners = [sibling, across] + y_others + z_others + x_others
+    partners = [y_others[0], y_others[2], z_others[0], z_others[2], sibling, y_others[1], z_others[1]] + x_others + [across]
     for partner in partners:
         pl.semaphore_signal(barrier, inc=1, device_id=partner, device_id_type=MESH)
     pl.semaphore_wait(barrier, len(partners))
@@ -67,15 +69,21 @@
     def piece(h, r, half, n=1):
         return gathered[h].at[pl.ds(r * 4 + 2 * half, 2 * n)]
 
-    def send(key, h, r, half, target, src=None, n=1, cond=None):
-        dst = piece(h, r, half, n)
+    def is_late(h, g):
+        return h == 1 and g >= 2
+
+    def late_piece(g, core, half, n=1):
+        return g_late.at[pl.ds(((g - 2) * 2 + core) * 4 + 2 * half, 2 * n)]
+
+    def send(key, h, r, half, target, src=None, n=1, cond=None, dst=None):
+        dst = piece(h, r, half, n) if dst is None else dst
         sem = send_g.at[h, slots.setdefault((h, key), sum(k[0] == h for k in slots))]
         copy = remote(dst if src is None else src, dst, sem, recv_g.at[h, r, half], target)
         copy.start()
-        waits[(h, key)] = (n, cond)
-
-    def arrive(h, r, half, n=1):
-        ref = piece(h, r, half, n)
+        waits[(h, key)] = (int(2 * n), cond)
+
+    def arrive(h, r, half, n=1, ref=None):
+        ref = piece(h, r, half, n) if ref is None else ref
         remote(ref, ref, send_g.at[h, 0], recv_g.at[h, r, half], sibling).wait_recv()
 
     def own_part(h, half, n=1):
@@ -119,24 +127,47 @@
         r_left = rows_of(sources[g], ring(y, -1), c)
         r_right = rows_of(sources[g], ring(y, 1), c)
         arrive(h, r_left, 0)
-        send(("y_y", g, 0), h, r_left, 0, right)
+        forward(("y_y", g, 0), h, g, r_left, 0, right)
         arrive(h, r_right, 1)
-        send(("y_y", g, 1), h, r_right, 1, left)
+        forward(("y_y", g, 1), h, g, r_right, 1, left)
         arrive(h, r_left, 1)
         send(("y_s", g, 0), h, r_left, 0, sibling, n=2)
         arrive(h, r_right, 0)
         send(("y_s", g, 1), h, r_right, 0, sibling, n=2)
 
+    def by_z(h, g):
+        return g == 1 and False
+
+    partner = at_rows(z + 1 - 2 * lax.rem(z, 2), y, c)
+
+    def part_of(h, r, k, n):
+        return gathered[h].at[pl.ds(r * 4 + k, n)]
+
+    def forward(key, h, g, r, half, target):
+        src = piece(h, r, half) if not by_z(h, g) else part_of(h, r, 3 * half, 1)
+        dst = late_piece(g, c, half) if is_late(h, g) else src
+        send(key, h, r, half, target, src=src, dst=dst, n=0.5 if by_z(h, g) else 1)
+
     def from_far(h, g, is_inner):
         r = rows_of(sources[g], ring(y, 2), c)
         for half in (0, 1):
-            arrive(h, r, half)
-        send(("f_s", g), h, r, 0, sibling, n=2)
-
-    def from_sibling(h):
-        for zs in range(RING):
-            for ys in range(RING):
-                arrive(h, rows_of(zs, ys, 1 - c), 0, 2)
+            ref = late_piece(g, c, half) if is_late(h, g) else None
+            arrive(h, r, half, ref=part_of(h, r, 3 * half, 1) if by_z(h, g) else ref)
+        middle = part_of(h, r, 1, 2)
+        if g == 0 and by_z(h, 1):
+            send(("f_z",), h, r, 2, partner, src=middle, dst=middle)
+        if by_z(h, g):
+            arrive(h, r, 2, ref=middle)
+        whole = late_piece(g, c, 0, 2) if is_late(h, g) else None
+        send(("f_s", g), h, r, 0, sibling, n=2, src=whole, dst=whole)
+
+    def from_sibling(h, late):
+        for g in range(RING):
+            for d in range(RING):
+                if late != (is_late(h, g) and d == 2):
+                    continue
+                ref = late_piece(g, 1 - c, 0, 2) if late else None
+                arrive(h, rows_of(sources[g], ring(y, d), 1 - c), 0, 2, ref)
 
     def local_part(h):
         copy = pltpu.make_async_copy(
@@ -183,29 +214,74 @@
         for d in range(3):
             send_low_to(("onward", d, part), j_across, x_others[d], None, part)
 
-    def low_finish():
-        own_low.wait()
+    def low_arrive(zhs):
         for part in range(LOW_PARTS):
             for d in (1, 2, 3):
-                arrive_low(zh * RING + ring(x, d), part)
-            for d in (1, 2, 3):
-                arrive_low((1 - zh) * RING + ring(x, d), part)
-
-    def low_turn(j):
-        low_t[pl.ds(j * BLK, BLK), :] = low_buf[j].T
+                arrive_low(zhs * RING + ring(x, d), part)
+
+    def low_turn(zhs):
+        for i in range(RING):
+            j = zhs * RING + i
+            low_t[pl.ds(pl.multiple_of(j * BLK, BLK), BLK), :] = low_buf[j].T
+
+    def place_of(b):
+        col = cols[rw * 64 + b]
+        chip = lax.shift_right_logical(col, 3)
+        late_2 = chip == sources[2] * RING + ring(y, 2)
+        late_3 = chip == sources[3] * RING + ring(y, 2)
+        return col, jnp.logical_or(late_2, late_3), jnp.bitwise_and(col, 7) + 8 * late_3.astype(jnp.int32)
+
+    def block_of(h, b):
+        col, late, _ = place_of(b)
+        return gathered[h][col if h == 0 else jnp.where(late, 128, col)]
 
     def apply_rows(h, q):
         def some(i, total):
             b = q * 16 + i * GROUP
             lhs = jnp.concatenate([d_buf[b + k] for k in range(GROUP)], axis=1)
-            rhs = jnp.concatenate([gathered[h][cols[rw * 64 + b + k]] for k in range(GROUP)], axis=0)
+            rhs = jnp.concatenate([block_of(h, b + k) for k in range(GROUP)], axis=0)
             return total + jnp.dot(lhs, rhs, preferred_element_type=jnp.float32)
 
         total = lax.fori_loop(0, 16 // GROUP, some, jnp.zeros((BLK, LANES), jnp.float32))
-        applied[h, pl.ds(q * BLK, BLK), :] = total.astype(jnp.bfloat16)
-
-    quarters = [ring(z, d) for d in (2, 3, 1, 0)]
-    quarter_shift = (2, 3, 1)
+        if h == 0:
+            applied[h, pl.ds(q * BLK, BLK), :] = total.astype(jnp.bfloat16)
+        else:
+            early[pl.ds(q * BLK, BLK), :] = total
+
+    def list_late():
+        def one(b, carry):
+            count, found = carry[0], carry[1:]
+            _, late, _ = place_of(b)
+            found = tuple(jnp.where(jnp.logical_and(late, count == i), b, f) for i, f in enumerate(found))
+            return (count + late.astype(jnp.int32),) + found
+
+        carry = (jnp.int32(0),) + (jnp.int32(0),) * LATE
+        for q in range(4):
+            late_list[LATE + q] = jnp.minimum(carry[0], LATE)
+            carry = lax.fori_loop(16 * q, 16 * q + 16, one, carry)
+        late_list[LATE + 4] = jnp.minimum(carry[0], LATE)
+        for i in range(LATE):
+            late_list[i] = carry[1 + i]
+
+    def apply_late():
+        late_parts[0] = jnp.zeros((BLK, LANES), jnp.float32)
+
+        def one(i, total):
+            for k in range(4):
+                b = jnp.bitwise_and(late_list[4 * i + k], 63)
+                _, _, at = place_of(b)
+                total = total + jnp.dot(d_buf[b], g_late[at], preferred_element_type=jnp.float32)
+                late_parts[4 * i + k + 1] = total
+            return total
+
+        lax.fori_loop(0, LATE // 4, one, jnp.zeros((BLK, LANES), jnp.float32))
+        for q in range(4):
+            here = pl.ds(q * BLK, BLK)
+            first, last = (jnp.clip(late_list[LATE + q + k], 0, LATE) for k in (0, 1))
+            total = early[here, :] + (late_parts[last] - late_parts[first])
+            applied[1, here, :] = total.astype(jnp.bfloat16)
+
+    quarters = [3 - z, jnp.where(z < 2, z + 2, z - 2), z + 1 - 2 * lax.rem(z, 2), z]
 
     def sum_copy(h, k, src, dst, target):
         return remote(src, dst, send_sum.at[h, k], recv_sum.at[h, k], target)
@@ -218,13 +294,14 @@
         return sum_copy(h, 3 + 3 * i + d, y_send.at[h, d, i], y_recv.at[h, d, i], y_others[d - 1])
 
     def z_copy(h, i):
-        return sum_copy(h, 16 + i, z_send.at[h, i], z_recv.at[h, i], z_others[quarter_shift[i] - 1])
-
-    def tile_quarter(h, i):
+        return sum_copy(h, 16 + i, z_send.at[h, i], z_recv.at[h, i], at_rows(quarters[i], y, c))
+
+    def tile_quarter(h, i, start=True):
         rows = pl.ds(pl.multiple_of(quarters[i] * 512, 512), 512)
         part = jnp.dot(low_t[rows, :], applied[h], preferred_element_type=jnp.float32)
         tiles[h][pl.ds(4 * quarters[i], 4)] = part.reshape(4, 2, 64, LANES)
-        sib_copy(h, i).start()
+        if start:
+            sib_copy(h, i).start()
 
     def y_quarter(h, i):
         sib_copy(h, i).wait()
@@ -234,8 +311,9 @@
             y_copy(h, i, d).start()
 
     def z_quarter(h, i):
-        for d in (1, 2, 3):
-            y_copy(h, i, d).wait()
+        if h == 1:
+            for d in (1, 2, 3):
+                y_copy(h, i, d).wait()
         p = quarters[i] * 4 + y
         total = tiles[h][p, c] + sib_buf[h, p]
         for d in (1, 2, 3):
@@ -245,12 +323,40 @@
         z_send[h, i] = total.astype(Z_TYPE)
         z_copy(h, i).start()
 
+    def sib_whole():
+        return sum_copy(0, 0, tiles[0].at[:, 1 - c], sib_buf.at[0], sibling)
+
+    def y_whole(d):
+        return sum_copy(0, 3 + d, y_send.at[0, d], y_recv.at[0, d], y_others[d - 1])
+
+    def tile_whole():
+        for i in range(4):
+            tile_quarter(0, i, False)
+        sib_whole().start()
+
+    def y_whole_fill():
+        sib_whole().wait()
+        for d in (2, 1, 3):
+            for i in range(4):
+                p = quarters[i] * 4 + ring(y, d)
+                y_send[0, d, i] = (tiles[0][p, c] + sib_buf[0, p]).astype(Y_TYPE)
+
+    def y_whole_start():
+        for d in (2, 1, 3):
+            y_whole(d).start()
+
+    def y_whole_wait():
+        for d in (2, 1, 3):
+            y_whole(d).wait()
+
     def sum_end(h, total):
         for i in range(3):
             z_copy(h, i).wait()
             total = total + z_recv[h, i].astype(jnp.float32)
         out[:, LANES * h : LANES * (h + 1)] = total
 
+    cols_copy = pltpu.make_async_copy(cols_all, cols, local_sem.at[4])
+    cols_copy.start()
     by_place([(own_z, 0), (own_y, 0)], [(own_z, 0), (own_y, 0)])
     local_0 = local_part(0)
     low_x(None)
@@ -258,20 +364,27 @@
     own_low.start()
     dip_copy = pltpu.make_async_copy(dip, d_buf, local_sem.at[3])
     dip_copy.start()
-    cols_copy = pltpu.make_async_copy(cols_all, cols, local_sem.at[4])
-    cols_copy.start()
     local_1 = local_part(1)
+    gathered[1][128] = jnp.zeros((BLK, LANES), jnp.bfloat16)
+    cols_copy.wait()
+    list_late()
     by_place(
         [(from_two, 0, 1), (low_across, 0), (from_y, 0, 0), (from_z, 0, 3), (low_across, 1), (low_across, 2), (from_y, 0, 1), (from_far, 0, 0),
-         (from_y, 0, 2), (own_y, 1), (own_z, 1), (low_onward, 0), (from_far, 0, 1), (from_y, 0, 3), (low_onward, 1), (from_far, 0, 2), (from_two, 1, 1), (from_far, 0, 3)],
+         (from_y, 0, 2), (own_y, 1), (own_z, 1), (low_across, 3), (low_onward, 0), (from_far, 0, 1)],
         [(from_z, 0, 1), (from_y, 0, 0), (from_y, 0, 1), (from_z, 0, 2), (low_across, 0), (from_far, 0, 0), (from_z, 0, 3), (low_across, 1), (low_across, 2),
-         (from_y, 0, 2), (from_far, 0, 1), (own_y, 1), (own_z, 1), (low_onward, 0), (from_y, 0, 3), (low_onward, 1), (from_far, 0, 2), (from_z, 1, 1), (from_far, 0, 3)],
+         (from_y, 0, 2), (from_far, 0, 1), (own_y, 1), (own_z, 1), (low_across, 3), (low_onward, 0)],
     )
-    from_sibling(0)
+    own_low.wait()
+    low_arrive(zh)
+    low_turn(zh)
+    by_place(
+        [(from_y, 0, 3), (low_onward, 1), (from_far, 0, 2), (from_two, 1, 1), (from_far, 0, 3)],
+        [(from_y, 0, 3), (low_onward, 1), (from_far, 0, 2), (from_z, 1, 1), (from_far, 0, 3)],
+    )
+    from_sibling(0, False)
     local_0.wait()
     dip_copy.wait()
-    cols_copy.wait()
-    by_place([(from_y, 1, 0), (low_across, 3), (low_onward, 2), (from_z, 1, 3)], [(from_y, 1, 0), (low_onward, 2), (from_z, 1, 2), (low_across, 3)])
+    by_place([(from_y, 1, 0), (low_onward, 2), (from_z, 1, 3)], [(from_y, 1, 0), (low_onward, 2), (from_z, 1, 2)])
     apply_rows(0, 0)
     apply_rows(0, 1)
     by_place([(from_y, 1, 1)], [(from_y, 1, 1)])
@@ -280,42 +393,45 @@
     by_place([(from_far, 1, 0)], [(from_z, 1, 3), (from_far, 1, 0)])
     low_onward(3, None)
     by_place([(from_y, 1, 2)], [(from_y, 1, 2)])
-    low_finish()
-    for j in range(8):
-        low_turn(j)
-    for i in range(4):
-        tile_quarter(0, i)
     by_place([(from_far, 1, 1)], [(from_far, 1, 1)])
-    for i in range(4):
-        y_quarter(0, i)
+    low_arrive(1 - zh)
+    low_turn(1 - zh)
     by_place([(from_y, 1, 3)], [(from_y, 1, 3)])
+    tile_whole()
+    y_whole_fill()
+    y_whole_start()
+    from_sibling(1, False)
+    local_1.wait()
+    apply_rows(1, 0)
+    apply_rows(1, 1)
     by_place([(from_far, 1, 2)], [(from_far, 1, 2)])
-    mine_0 = [z_quarter(0, i) for i in range(4)][3]
+    apply_rows(1, 2)
+    apply_rows(1, 3)
     by_place([(from_far, 1, 3)], [(from_far, 1, 3)])
-    from_sibling(1)
-    local_1.wait()
-    for q in range(4):
-        apply_rows(1, q)
+    from_sibling(1, True)
+    apply_late()
     tile_quarter(1, 0)
     tile_quarter(1, 1)
+    tile_quarter(1, 2)
     y_quarter(1, 0)
-    tile_quarter(1, 2)
     y_quarter(1, 1)
+    y_quarter(1, 2)
     tile_quarter(1, 3)
-    y_quarter(1, 2)
     y_quarter(1, 3)
-    sum_end(0, mine_0)
+    y_whole_wait()
+    mine_0 = [z_quarter(0, i) for i in range(4)][3]
     z_quarter(1, 0)
     z_quarter(1, 1)
     z_quarter(1, 2)
     mine_1 = z_quarter(1, 3)
+    sum_end(0, mine_0)
     for (h, key), (n, cond) in waits.items():
         slot = slots[(h, key)]
         if h == "low":
             ref = low_buf.at[0, pl.ds(0, 256)]
             copy = remote(ref, ref, send_low.at[slot], recv_low.at[0, 0], sibling)
         else:
-            ref = gathered[h].at[pl.ds(0, 2 * n)]
+            ref = gathered[h].at[pl.ds(0, n)]
             copy = remote(ref, ref, send_g.at[h, slot], recv_g.at[h, 0, 0], sibling)
         if cond is None:
             copy.wait_send()
@@ -333,7 +449,7 @@
         out_specs=pl.BlockSpec(memory_space=pltpu.VMEM),
         scratch_shapes=[
             pltpu.VMEM((128, BLK, LANES), jnp.bfloat16),
-            pltpu.VMEM((128, BLK, LANES), jnp.bfloat16),
+            pltpu.VMEM((129, BLK, LANES), jnp.bfloat16),
             pltpu.VMEM((64, BLK, BLK), jnp.bfloat16),
             pltpu.VMEM((8, 1024, 256), jnp.bfloat16),
             pltpu.VMEM((2048, 1024), jnp.bfloat16),
@@ -345,7 +461,7 @@
             pltpu.VMEM((2, 4, 4, 64, LANES), Y_TYPE),
             pltpu.VMEM((2, 4, 64, LANES), Z_TYPE),
             pltpu.VMEM((2, 4, 64, LANES), Z_TYPE),
-            pltpu.SemaphoreType.DMA((2, 32, 2)),
+            pltpu.SemaphoreType.DMA((2, 32, 3)),
             pltpu.SemaphoreType.DMA((2, 72)),
             pltpu.SemaphoreType.DMA((8, 4)),
             pltpu.SemaphoreType.DMA((32,)),
@@ -353,6 +469,10 @@
             pltpu.SemaphoreType.DMA((2, 20)),
             pltpu.SemaphoreType.DMA((5,)),
             pltpu.SMEM((2048,), jnp.int32),
+            pltpu.VMEM((LATE, BLK, LANES), jnp.bfloat16),
+            pltpu.VMEM((1024, LANES), jnp.float32),
+            pltpu.VMEM((LATE + 1, BLK, LANES), jnp.float32),
+            pltpu.SMEM((LATE + 5,), jnp.int32),
         ],
         compiler_params=pltpu.CompilerParams(
             collective_id=0, has_side_effects=True, vmem_limit_bytes=56 * 1024 * 1024

time: 109 us -> 103 us (0.945)
  Pallas kernels: 107 us -> 101 us
    pallas_call x1, Pallas kernels: 107 us -> 101 us  [shards(): pl.pallas_call(kernel, out_shape=jax.ShapeDtypeStruct((64, 256), jnp.floa...]
where the time goes in v5:
time: 103 us
  Pallas kernels  101 us (98%)
  local copies, waits for them, and re-layouts  1.47 us (1%)
    pallas_call x1, Pallas kernels, shards(): pl.pallas_call(kernel, out_shape=jax.ShapeDtypeStruct((64, 256), jnp.floa...  101 us

profile of v5, /device:TPU:1, one launch (start us, length us, event | category | flops | bytes accessed | tf_op | source)
XLA Modules:
  0.0 103.0 jit_solution(12799064950780343720)
XLA Ops:
  0.0 101.5 %shard_map.46 = f32[64,256]{1,0:T(8,128)} custom-call(s32[2048]{0:T(1024)} %cols_all.1, bf16[1024,256]{1,0:T(8,128)(2,1)} %low.1, bf16[4,256,256]{2,1,0:T(8,128)(2,1)} %bitcast.1, bf16[64,256,256]{2,1,0:T(8,128)(2,1)} %dip.1), custom_call_target="tpu_custom_call" | custom-call | flops 3221225472 | bytes 10485760 | tf_op jit(solution)/shard_map/pallas_call | solution.py:445
  101.5 1.5 %copy.6 = f32[64,256]{1,0:T(8,128)} copy(f32[64,256]{1,0:T(8,128)} %shard_map.46) | data formatting | bytes 131072

commit v6 on v5

--- a/solution.py
+++ b/solution.py
@@ -21,7 +21,7 @@
     cols_all, low, high, dip, out,
     g_a, g_b, d_buf, low_buf, low_t, applied, tile_a, tile_b, sib_buf, y_send, y_recv, z_send, z_recv,
     recv_g, send_g, recv_low, send_low, recv_sum, send_sum, local_sem, cols,
-    g_late, early, late_parts, late_list,
+    g_late, early, late_parts, late_list, across_here,
 ):
     gathered = (g_a, g_b)
     tiles = (tile_a, tile_b)
@@ -50,10 +50,19 @@
     across = at_jpair(1 - zh, x)
 
     barrier = pltpu.get_barrier_semaphore()
-    partners = [y_others[0], y_others[2], z_others[0], z_others[2], sibling, y_others[1], z_others[1]] + x_others + [across]
+    partners = [y_others[0], y_others[2], z_others[0], z_others[2], sibling, y_others[1], z_others[1]] + x_others
     for partner in partners:
         pl.semaphore_signal(barrier, inc=1, device_id=partner, device_id_type=MESH)
-    pl.semaphore_wait(barrier, len(partners))
+
+    @pl.when(zh == 0)
+    def _():
+        pl.semaphore_signal(barrier, inc=1, device_id=across, device_id_type=MESH)
+        pl.semaphore_wait(barrier, len(partners))
+
+    @pl.when(zh == 1)
+    def _():
+        pl.semaphore_wait(barrier, len(partners) + 1)
+        pl.semaphore_signal(across_here, inc=1, device_id=across, device_id_type=MESH)
 
     waits = {}
 
@@ -136,7 +145,7 @@
         send(("y_s", g, 1), h, r_right, 0, sibling, n=2)
 
     def by_z(h, g):
-        return g == 1 and False
+        return g == 1 and h == 1
 
     partner = at_rows(z + 1 - 2 * lax.rem(z, 2), y, c)
 
@@ -207,6 +216,12 @@
                 send_low_to(("x", d, part), jp, x_others[d], low.at[pl.ds(part * 256, 256)], part)
 
     def low_across(part, is_inner):
+        if part == 0:
+
+            @pl.when(zh == 0)
+            def _():
+                pl.semaphore_wait(across_here, 1)
+
         send_low_to(("across", part), jp, across, low.at[pl.ds(part * 256, 256)], part)
 
     def low_onward(part, is_inner):
@@ -220,9 +235,12 @@
                 arrive_low(zhs * RING + ring(x, d), part)
 
     def low_turn(zhs):
-        for i in range(RING):
+        def one(i, _):
             j = zhs * RING + i
             low_t[pl.ds(pl.multiple_of(j * BLK, BLK), BLK), :] = low_buf[j].T
+            return 0
+
+        lax.fori_loop(0, RING, one, 0)
 
     def place_of(b):
         col = cols[rw * 64 + b]
@@ -235,18 +253,23 @@
         col, late, _ = place_of(b)
         return gathered[h][col if h == 0 else jnp.where(late, 128, col)]
 
-    def apply_rows(h, q):
-        def some(i, total):
-            b = q * 16 + i * GROUP
-            lhs = jnp.concatenate([d_buf[b + k] for k in range(GROUP)], axis=1)
-            rhs = jnp.concatenate([block_of(h, b + k) for k in range(GROUP)], axis=0)
-            return total + jnp.dot(lhs, rhs, preferred_element_type=jnp.float32)
-
-        total = lax.fori_loop(0, 16 // GROUP, some, jnp.zeros((BLK, LANES), jnp.float32))
-        if h == 0:
-            applied[h, pl.ds(q * BLK, BLK), :] = total.astype(jnp.bfloat16)
-        else:
-            early[pl.ds(q * BLK, BLK), :] = total
+    def apply_rows(h, q0, n):
+        def row(q, _):
+            def some(i, total):
+                b = q * 16 + i * GROUP
+                lhs = jnp.concatenate([d_buf[b + k] for k in range(GROUP)], axis=1)
+                rhs = jnp.concatenate([block_of(h, b + k) for k in range(GROUP)], axis=0)
+                return total + jnp.dot(lhs, rhs, preferred_element_type=jnp.float32)
+
+            total = lax.fori_loop(0, 16 // GROUP, some, jnp.zeros((BLK, LANES), jnp.float32))
+            here = pl.ds(pl.multiple_of(q * BLK, BLK), BLK)
+            if h == 0:
+                applied[h, here, :] = total.astype(jnp.bfloat16)
+            else:
+                early[here, :] = total
+            return 0
+
+        lax.fori_loop(q0, q0 + n, row, 0)
 
     def list_late():
         def one(b, carry):
@@ -296,12 +319,18 @@
     def z_copy(h, i):
         return sum_copy(h, 16 + i, z_send.at[h, i], z_recv.at[h, i], at_rows(quarters[i], y, c))
 
-    def tile_quarter(h, i, start=True):
-        rows = pl.ds(pl.multiple_of(quarters[i] * 512, 512), 512)
-        part = jnp.dot(low_t[rows, :], applied[h], preferred_element_type=jnp.float32)
-        tiles[h][pl.ds(4 * quarters[i], 4)] = part.reshape(4, 2, 64, LANES)
-        if start:
-            sib_copy(h, i).start()
+    def tile_quarters(h, i0, n):
+        def one(i, _):
+            quarter = jnp.where(i < 2, jnp.where(i == 0, quarters[0], quarters[1]), jnp.where(i == 2, quarters[2], z))
+            rows = pl.ds(pl.multiple_of(quarter * 512, 512), 512)
+            part = jnp.dot(low_t[rows, :], applied[h], preferred_element_type=jnp.float32)
+            tiles[h][pl.ds(4 * quarter, 4)] = part.reshape(4, 2, 64, LANES)
+            if h == 1:
+                at = pl.ds(4 * quarter, 4)
+                sum_copy(h, i, tiles[h].at[at, 1 - c], sib_buf.at[h, at], sibling).start()
+            return 0
+
+        lax.fori_loop(i0, i0 + n, one, 0)
 
     def y_quarter(h, i):
         sib_copy(h, i).wait()
@@ -330,8 +359,7 @@
         return sum_copy(0, 3 + d, y_send.at[0, d], y_recv.at[0, d], y_others[d - 1])
 
     def tile_whole():
-        for i in range(4):
-            tile_quarter(0, i, False)
+        tile_quarters(0, 0, 4)
         sib_whole().start()
 
     def y_whole_fill():
@@ -385,11 +413,9 @@
     local_0.wait()
     dip_copy.wait()
     by_place([(from_y, 1, 0), (low_onward, 2), (from_z, 1, 3)], [(from_y, 1, 0), (low_onward, 2), (from_z, 1, 2)])
-    apply_rows(0, 0)
-    apply_rows(0, 1)
+    apply_rows(0, 0, 2)
     by_place([(from_y, 1, 1)], [(from_y, 1, 1)])
-    apply_rows(0, 2)
-    apply_rows(0, 3)
+    apply_rows(0, 2, 2)
     by_place([(from_far, 1, 0)], [(from_z, 1, 3), (from_far, 1, 0)])
     low_onward(3, None)
     by_place([(from_y, 1, 2)], [(from_y, 1, 2)])
@@ -402,21 +428,17 @@
     y_whole_start()
     from_sibling(1, False)
     local_1.wait()
-    apply_rows(1, 0)
-    apply_rows(1, 1)
+    apply_rows(1, 0, 2)
     by_place([(from_far, 1, 2)], [(from_far, 1, 2)])
-    apply_rows(1, 2)
-    apply_rows(1, 3)
+    apply_rows(1, 2, 2)
     by_place([(from_far, 1, 3)], [(from_far, 1, 3)])
     from_sibling(1, True)
     apply_late()
-    tile_quarter(1, 0)
-    tile_quarter(1, 1)
-    tile_quarter(1, 2)
+    tile_quarters(1, 0, 3)
     y_quarter(1, 0)
     y_quarter(1, 1)
     y_quarter(1, 2)
-    tile_quarter(1, 3)
+    tile_quarters(1, 3, 1)
     y_quarter(1, 3)
     y_whole_wait()
     mine_0 = [z_quarter(0, i) for i in range(4)][3]
@@ -444,7 +466,7 @@
     any_space = pl.BlockSpec(memory_space=pl.ANY)
     return pl.pallas_call(
         kernel,
-        out_shape=jax.ShapeDtypeStruct((64, 256), jnp.float32),
+        out_shape=pltpu.VMEM((64, 256), jnp.float32),
         in_specs=[any_space] * 4,
         out_specs=pl.BlockSpec(memory_space=pltpu.VMEM),
         scratch_shapes=[
@@ -473,6 +495,7 @@
             pltpu.VMEM((1024, LANES), jnp.float32),
             pltpu.VMEM((LATE + 1, BLK, LANES), jnp.float32),
             pltpu.SMEM((LATE + 5,), jnp.int32),
+            pltpu.SemaphoreType.REGULAR,
         ],
         compiler_params=pltpu.CompilerParams(
             collective_id=0, has_side_effects=True, vmem_limit_bytes=56 * 1024 * 1024

time: 103 us -> 98.7 us (0.958)
  Pallas kernels: 101 us -> 97.9 us
    pallas_call x1, Pallas kernels: 101 us -> 97.9 us  [shards(): pl.pallas_call(kernel, out_shape=pltpu.VMEM((64, 256), jnp.float32), in_s...]
where the time goes in v6:
time: 98.7 us; the launch traced here: 98.6 us
  Pallas kernels  97.9 us (99%)
    pallas_call x1, Pallas kernels, shards(): pl.pallas_call(kernel, out_shape=pltpu.VMEM((64, 256), jnp.float32), in_s...  97.9 us

profile of v6, /device:TPU:1, one launch (start us, length us, event | category | flops | bytes accessed | tf_op | source)
XLA Modules:
  0.0 98.6 jit_solution(3354782080066401249)
XLA Ops:
  0.0 97.9 %shard_map.46 = f32[64,256]{1,0:T(8,128)S(1)} custom-call(s32[2048]{0:T(1024)} %cols_all.1, bf16[1024,256]{1,0:T(8,128)(2,1)} %low.1, bf16[4,256,256]{2,1,0:T(8,128)(2,1)} %bitcast.1, bf16[64,256,256]{2,1,0:T(8,128)(2,1)} %dip.1), custom_call_target="tpu_custom_call" | custom-call | flops 3221225472 | bytes 10485760 | tf_op jit(solution)/shard_map/pallas_call | solution.py:467
  97.9 0.6 copy.6

commit v7 on v6

--- a/solution.py
+++ b/solution.py
@@ -319,9 +319,9 @@
     def z_copy(h, i):
         return sum_copy(h, 16 + i, z_send.at[h, i], z_recv.at[h, i], at_rows(quarters[i], y, c))
 
-    def tile_quarters(h, i0, n):
+    def tile_quarters(h, i0, n, first=None):
         def one(i, _):
-            quarter = jnp.where(i < 2, jnp.where(i == 0, quarters[0], quarters[1]), jnp.where(i == 2, quarters[2], z))
+            quarter = first + i if h == 0 else jnp.where(i < 2, jnp.where(i == 0, quarters[0], quarters[1]), jnp.where(i == 2, quarters[2], z))
             rows = pl.ds(pl.multiple_of(quarter * 512, 512), 512)
             part = jnp.dot(low_t[rows, :], applied[h], preferred_element_type=jnp.float32)
             tiles[h][pl.ds(4 * quarter, 4)] = part.reshape(4, 2, 64, LANES)
@@ -358,9 +358,8 @@
     def y_whole(d):
         return sum_copy(0, 3 + d, y_send.at[0, d], y_recv.at[0, d], y_others[d - 1])
 
-    def tile_whole():
-        tile_quarters(0, 0, 4)
-        sib_whole().start()
+    def tile_half(zhs):
+        tile_quarters(0, 0, 2, 2 * zhs)
 
     def y_whole_fill():
         sib_whole().wait()
@@ -416,6 +415,7 @@
     apply_rows(0, 0, 2)
     by_place([(from_y, 1, 1)], [(from_y, 1, 1)])
     apply_rows(0, 2, 2)
+    tile_half(zh)
     by_place([(from_far, 1, 0)], [(from_z, 1, 3), (from_far, 1, 0)])
     low_onward(3, None)
     by_place([(from_y, 1, 2)], [(from_y, 1, 2)])
@@ -423,12 +423,13 @@
     low_arrive(1 - zh)
     low_turn(1 - zh)
     by_place([(from_y, 1, 3)], [(from_y, 1, 3)])
-    tile_whole()
-    y_whole_fill()
-    y_whole_start()
+    tile_half(1 - zh)
+    sib_whole().start()
     from_sibling(1, False)
     local_1.wait()
     apply_rows(1, 0, 2)
+    y_whole_fill()
+    y_whole_start()
     by_place([(from_far, 1, 2)], [(from_far, 1, 2)])
     apply_rows(1, 2, 2)
     by_place([(from_far, 1, 3)], [(from_far, 1, 3)])

time: 98.7 us -> 97.7 us (0.990)
  Pallas kernels: 97.9 us -> 96.9 us
    pallas_call x1, Pallas kernels: 97.9 us -> 96.9 us  [shards(): pl.pallas_call(kernel, out_shape=pltpu.VMEM((64, 256), jnp.float32), in_s...]
where the time goes in v7:
time: 97.7 us; the launch traced here: 97.5 us
  Pallas kernels  96.9 us (99%)
    pallas_call x1, Pallas kernels, shards(): pl.pallas_call(kernel, out_shape=pltpu.VMEM((64, 256), jnp.float32), in_s...  96.9 us

profile of v7, /device:TPU:1, one launch (start us, length us, event | category | flops | bytes accessed | tf_op | source)
XLA Modules:
  0.0 97.5 jit_solution(16619915188497273728)
XLA Ops:
  0.0 96.9 %shard_map.46 = f32[64,256]{1,0:T(8,128)S(1)} custom-call(s32[2048]{0:T(1024)} %cols_all.1, bf16[1024,256]{1,0:T(8,128)(2,1)} %low.1, bf16[4,256,256]{2,1,0:T(8,128)(2,1)} %bitcast.1, bf16[64,256,256]{2,1,0:T(8,128)(2,1)} %dip.1), custom_call_target="tpu_custom_call" | custom-call | flops 3221225472 | bytes 10485760 | tf_op jit(solution)/shard_map/pallas_call | solution.py:468
  96.9 0.6 copy.6

commit v8 on v7

--- a/solution.py
+++ b/solution.py
@@ -411,9 +411,9 @@
     from_sibling(0, False)
     local_0.wait()
     dip_copy.wait()
-    by_place([(from_y, 1, 0), (low_onward, 2), (from_z, 1, 3)], [(from_y, 1, 0), (low_onward, 2), (from_z, 1, 2)])
+    by_place([(from_y, 1, 0), (low_onward, 2)], [(from_y, 1, 0), (low_onward, 2)])
     apply_rows(0, 0, 2)
-    by_place([(from_y, 1, 1)], [(from_y, 1, 1)])
+    by_place([(from_y, 1, 1), (from_z, 1, 3)], [(from_y, 1, 1), (from_z, 1, 2)])
     apply_rows(0, 2, 2)
     tile_half(zh)
     by_place([(from_far, 1, 0)], [(from_z, 1, 3), (from_far, 1, 0)])

time: 97.7 us -> 96.2 us (0.985)
  Pallas kernels: 96.9 us -> 95.4 us
    pallas_call x1, Pallas kernels: 96.9 us -> 95.4 us  [shards(): pl.pallas_call(kernel, out_shape=pltpu.VMEM((64, 256), jnp.float32), in_s...]
where the time goes in v8:
time: 96.2 us; the launch traced here: 96.1 us
  Pallas kernels  95.4 us (99%)
    pallas_call x1, Pallas kernels, shards(): pl.pallas_call(kernel, out_shape=pltpu.VMEM((64, 256), jnp.float32), in_s...  95.4 us

profile of v8, /device:TPU:1, one launch (start us, length us, event | category | flops | bytes accessed | tf_op | source)
XLA Modules:
  0.0 96.1 jit_solution(7943896016999954927)
XLA Ops:
  0.0 95.4 %shard_map.46 = f32[64,256]{1,0:T(8,128)S(1)} custom-call(s32[2048]{0:T(1024)} %cols_all.1, bf16[1024,256]{1,0:T(8,128)(2,1)} %low.1, bf16[4,256,256]{2,1,0:T(8,128)(2,1)} %bitcast.1, bf16[64,256,256]{2,1,0:T(8,128)(2,1)} %dip.1), custom_call_target="tpu_custom_call" | custom-call | flops 3221225472 | bytes 10485760 | tf_op jit(solution)/shard_map/pallas_call | solution.py:468
  95.4 0.6 copy.6

commit v9 on v8

--- a/solution.py
+++ b/solution.py
@@ -21,7 +21,7 @@
     cols_all, low, high, dip, out,
     g_a, g_b, d_buf, low_buf, low_t, applied, tile_a, tile_b, sib_buf, y_send, y_recv, z_send, z_recv,
     recv_g, send_g, recv_low, send_low, recv_sum, send_sum, local_sem, cols,
-    g_late, early, late_parts, late_list, across_here,
+    g_late, early, late_parts, late_list, across_here, higher_here,
 ):
     gathered = (g_a, g_b)
     tiles = (tile_a, tile_b)
@@ -50,19 +50,38 @@
     across = at_jpair(1 - zh, x)
 
     barrier = pltpu.get_barrier_semaphore()
-    partners = [y_others[0], y_others[2], z_others[0], z_others[2], sibling, y_others[1], z_others[1]] + x_others
+    partners = [y_others[0], y_others[2], sibling, y_others[1]] + x_others
     for partner in partners:
         pl.semaphore_signal(barrier, inc=1, device_id=partner, device_id_type=MESH)
+
+    for zs in range(1, RING):
+
+        @pl.when(zs > z)
+        def _(zs=zs):
+            pl.semaphore_signal(barrier, inc=1, device_id=at_rows(zs, y, c), device_id_type=MESH)
 
     @pl.when(zh == 0)
     def _():
         pl.semaphore_signal(barrier, inc=1, device_id=across, device_id_type=MESH)
-        pl.semaphore_wait(barrier, len(partners))
+        pl.semaphore_wait(barrier, len(partners) + z)
 
     @pl.when(zh == 1)
     def _():
-        pl.semaphore_wait(barrier, len(partners) + 1)
+        pl.semaphore_wait(barrier, len(partners) + 1 + z)
         pl.semaphore_signal(across_here, inc=1, device_id=across, device_id_type=MESH)
+
+    for zs in range(RING - 1):
+
+        @pl.when(zs < z)
+        def _(zs=zs):
+            pl.semaphore_signal(higher_here.at[z], inc=1, device_id=at_rows(zs, y, c), device_id_type=MESH)
+
+    def wait_higher(first, last):
+        for zs in range(1, RING):
+
+            @pl.when(jnp.logical_and(zs >= z + first, zs <= z + last))
+            def _(zs=zs):
+                pl.semaphore_wait(higher_here.at[zs], 1)
 
     waits = {}
 
@@ -384,7 +403,9 @@
 
     cols_copy = pltpu.make_async_copy(cols_all, cols, local_sem.at[4])
     cols_copy.start()
-    by_place([(own_z, 0), (own_y, 0)], [(own_z, 0), (own_y, 0)])
+    by_place([(own_y, 0)], [(own_y, 0)])
+    wait_higher(1, 1)
+    by_place([(own_z, 0)], [(own_z, 0)])
     local_0 = local_part(0)
     low_x(None)
     own_low = pltpu.make_async_copy(low, low_buf.at[jp], local_sem.at[2])
@@ -408,6 +429,7 @@
         [(from_y, 0, 3), (low_onward, 1), (from_far, 0, 2), (from_two, 1, 1), (from_far, 0, 3)],
         [(from_y, 0, 3), (low_onward, 1), (from_far, 0, 2), (from_z, 1, 1), (from_far, 0, 3)],
     )
+    wait_higher(2, 3)
     from_sibling(0, False)
     local_0.wait()
     dip_copy.wait()
@@ -497,6 +519,7 @@
             pltpu.VMEM((LATE + 1, BLK, LANES), jnp.float32),
             pltpu.SMEM((LATE + 5,), jnp.int32),
             pltpu.SemaphoreType.REGULAR,
+            pltpu.SemaphoreType.REGULAR((RING,)),
         ],
         compiler_params=pltpu.CompilerParams(
             collective_id=0, has_side_effects=True, vmem_limit_bytes=56 * 1024 * 1024

time: 96.2 us -> 97.1 us (level)
  Pallas kernels: 95.4 us -> 96.4 us
where the time goes in v9:
time: 97.1 us; the launch traced here: 97 us
  Pallas kernels  96.4 us (99%)
    pallas_call x1, Pallas kernels, shards(): pl.pallas_call(kernel, out_shape=pltpu.VMEM((64, 256), jnp.float32), in_s...  96.4 us

profile of v9, /device:TPU:1, one launch (start us, length us, event | category | flops | bytes accessed | tf_op | source)
XLA Modules:
  0.0 97.0 jit_solution(16306789502648189495)
XLA Ops:
  0.0 96.4 %shard_map.46 = f32[64,256]{1,0:T(8,128)S(1)} custom-call(s32[2048]{0:T(1024)} %cols_all.1, bf16[1024,256]{1,0:T(8,128)(2,1)} %low.1, bf16[4,256,256]{2,1,0:T(8,128)(2,1)} %bitcast.1, bf16[64,256,256]{2,1,0:T(8,128)(2,1)} %dip.1), custom_call_target="tpu_custom_call" | custom-call | flops 3221225472 | bytes 10485760 | tf_op jit(solution)/shard_map/pallas_call | solution.py:490
  96.4 0.6 copy.6
